TPU v7x, 128 devices: a whole 4x4x4 slice. The times are simulated.
128 devices in a mesh: seq: 16 (over y, x_lo, core), fsdp: 8 (over x_hi, z).
Axes of the slice: x: 4 (x_hi: 2, x_lo: 2; x = x_hi * 2 + x_lo), y: 4, z: 4, core: 2. Of those that a mesh axis runs over, the one named last changes fastest.
Arguments:
- q_nope: bfloat16 [2048, 16384], P('seq', 'fsdp'), may hold values from -6 to 6
- q_rope: bfloat16 [2048, 8192], P('seq', 'fsdp'), may hold values from -8 to 8
- latent_t: bfloat16 [512, 2048], P(None, 'seq'), may hold values from -6 to 6
- k_rope_t: bfloat16 [64, 2048], P(None, 'seq'), may hold values from -8 to 8
- w_uk: bfloat16 [512, 16384], P('seq', 'fsdp'), may hold values from -0.25 to 0.25
- w_uv: bfloat16 [512, 16384], P('seq', 'fsdp'), may hold values from -0.25 to 0.25
- grad_out: bfloat16 [2048, 16384], P('seq', 'fsdp'), may hold values from -6 to 6
- seg_ids: int32 [2048], replicated, may hold values from 0 to 7, as said below
- anc_flags: int32 [16, 16], replicated, may hold values from 0 to 1, as said below
Outputs:
- attn_out: bfloat16 [2048, 16384], P('seq', 'fsdp')
- d_q_nope: bfloat16 [2048, 16384], P('seq', 'fsdp')
- d_q_rope: bfloat16 [2048, 8192], P('seq', 'fsdp')
- d_latent_t: bfloat16 [512, 2048], P(None, 'seq')
- d_k_rope_t: bfloat16 [64, 2048], P(None, 'seq')
- d_w_uk: float32 [512, 16384], P('seq', 'fsdp')
- d_w_uv: float32 [512, 16384], P('seq', 'fsdp')
Inputs may be any that keep to these rules, and one draw needn't show every extreme that they name: seg_ids start at 0, never fall, are constant over each aligned run of 128 tokens and rise by at most one from one run to the next; segment 0 is an ancestor of every other segment. anc_flags[a, b] is 1 exactly where the segment of block b is a strict ancestor of the segment of block a in a tree of segments whose parents come earlier, so only where b < a.
All inputs are finite; a program needn't handle non-finite values.
Results may differ from a plain program's by a relative error of at most 0.035.
Values may be sent and summed in bfloat16 or wider, within the bound.
A program may use at most 128 MiB of HBM per device.

v0:
```python
import math

import jax
import jax.numpy as jnp
from jax import lax
from jax.sharding import PartitionSpec as P

LATENT = 512
ROPE = 64
NOPE = 128
VDIM = 128
BLOCK = 128


NEG_FILL = -1e30


def contract_last(left, right):
    return lax.dot_general(
        left, right, (((1,), (1,)), ((), ())), preferred_element_type=jnp.float32
    )


def contract_first(left, right):
    return lax.dot_general(
        left, right, (((0,), (0,)), ((), ())), preferred_element_type=jnp.float32
    )


def sweep_blocks(step_fn, state_now, key_parts, first_key):
    lat_part, rope_part = key_parts
    key_count = lat_part.shape[1]
    span_len = math.gcd(key_count, BLOCK)

    def visit_block(block_num, state_in):
        offset = block_num * span_len
        lat_block = lax.dynamic_slice_in_dim(lat_part, offset, span_len, 1)
        rope_block = lax.dynamic_slice_in_dim(rope_part, offset, span_len, 1)
        return step_fn(state_in, lat_block, rope_block, first_key + offset)

    return lax.fori_loop(0, key_count // span_len, visit_block, state_now)


def unchanged(state_in):
    return state_in


def on_device(q_nope, q_rope, latent_t, k_rope_t, w_uk, w_uv, grad_out, seg_ids, anc_flags):
    tok_local = q_nope.shape[0]
    heads_here = q_nope.shape[1] // NOPE
    row_count = tok_local * heads_here
    total_tokens = seg_ids.shape[0]
    score_scale = 1.0 / math.sqrt(NOPE + ROPE)
    shard_id = lax.axis_index("seq")
    query_pos = shard_id * tok_local + jnp.arange(tok_local, dtype=jnp.int32)
    query_seg = lax.dynamic_slice_in_dim(seg_ids, shard_id * tok_local, tok_local)
    flag_rows = lax.dynamic_slice_in_dim(
        anc_flags, shard_id * (tok_local // BLOCK), tok_local // BLOCK, 0
    )
    nope3 = q_nope.reshape(tok_local, heads_here, NOPE)
    rope_rows = q_rope.reshape(row_count, ROPE)
    grad3 = grad_out.reshape(tok_local, heads_here, VDIM)

    def visibility(first_key, span_len):
        key_pos = first_key + jnp.arange(span_len, dtype=jnp.int32)
        key_seg = lax.dynamic_slice_in_dim(seg_ids, first_key, span_len)
        block_col = lax.dynamic_slice_in_dim(flag_rows, first_key // BLOCK, 1, 1)
        flag_tok = jnp.repeat(block_col[:, 0], BLOCK, total_repeat_length=tok_local)
        same_seg = (query_seg[:, None] == key_seg[None, :]) & (
            key_pos[None, :] <= query_pos[:, None]
        )
        return same_seg | (flag_tok[:, None] == 1)

    panels = (
        lax.all_gather(w_uk, "seq", axis=0, tiled=True),
        lax.all_gather(w_uv, "seq", axis=0, tiled=True),
    )
    uk_full = panels[0].reshape(LATENT, heads_here, NOPE)
    uv_full = panels[1].reshape(LATENT, heads_here, VDIM)
    q_abs3 = jnp.einsum("thn,lhn->thl", nope3, uk_full, preferred_element_type=jnp.float32).astype(
        jnp.bfloat16
    )
    query_rows = q_abs3.reshape(row_count, LATENT)

    def score_block(lat_block, rope_block):
        scores = (
            jnp.dot(query_rows, lat_block, preferred_element_type=jnp.float32)
            + jnp.dot(rope_rows, rope_block, preferred_element_type=jnp.float32)
        ) * score_scale
        return scores.reshape(tok_local, heads_here, -1)

    def statistics_step(state_now, lat_block, rope_block, first_key):
        visible = visibility(first_key, lat_block.shape[1])

        def statistics_compute(state_in):
            run_max, run_sum = state_in
            masked = jnp.where(visible[:, None, :], score_block(lat_block, rope_block), NEG_FILL)
            new_max = jnp.maximum(run_max, jnp.max(masked, axis=2))
            weights = jnp.where(visible[:, None, :], jnp.exp(masked - new_max[:, :, None]), 0.0)
            new_sum = run_sum * jnp.exp(run_max - new_max) + jnp.sum(weights, axis=2)
            return (new_max, new_sum)

        return lax.cond(jnp.any(visible), statistics_compute, unchanged, state_now)

    statistics_init = (
        jnp.full((tok_local, heads_here), NEG_FILL, jnp.float32),
        jnp.zeros((tok_local, heads_here), jnp.float32),
    )
    key_parts = (
        lax.all_gather(latent_t, "seq", axis=1, tiled=True),
        lax.all_gather(k_rope_t, "seq", axis=1, tiled=True),
    )
    run_max, run_sum = sweep_blocks(statistics_step, statistics_init, key_parts, 0)
    log_total = run_max + jnp.log(run_sum)

    def forward_step(accumulated, lat_block, rope_block, first_key):
        visible = visibility(first_key, lat_block.shape[1])

        def forward_compute(acc_in):
            scores = score_block(lat_block, rope_block)
            probabilities = jnp.where(
                visible[:, None, :], jnp.exp(scores - log_total[:, :, None]), 0.0
            )
            rounded = probabilities.astype(jnp.bfloat16).reshape(row_count, -1)
            return acc_in + contract_last(rounded, lat_block)

        return lax.cond(jnp.any(visible), forward_compute, unchanged, accumulated)

    forward_init = jnp.zeros((row_count, LATENT), jnp.float32)
    accumulated = sweep_blocks(forward_step, forward_init, key_parts, 0)
    o_lat_rows = accumulated.astype(jnp.bfloat16)
    o_lat3 = o_lat_rows.reshape(tok_local, heads_here, LATENT)
    attn3 = jnp.einsum("thl,lhv->thv", o_lat3, uv_full, preferred_element_type=jnp.float32)
    d_o_lat3 = jnp.einsum(
        "thv,lhv->thl", grad3, uv_full, preferred_element_type=jnp.float32
    ).astype(jnp.bfloat16)
    attn_out = attn3.astype(jnp.bfloat16).reshape(tok_local, heads_here * VDIM)
    d_o_rows = d_o_lat3.reshape(row_count, LATENT)
    row_delta = jnp.sum(d_o_lat3.astype(jnp.float32) * o_lat3.astype(jnp.float32), axis=2)

    def backward_step(state_now, lat_block, rope_block, first_key):
        span_len = lat_block.shape[1]
        visible = visibility(first_key, span_len)

        def backward_compute(state_in):
            grad_abs, grad_rope, grad_lat, grad_kr = state_in
            scores = score_block(lat_block, rope_block)
            probabilities = jnp.where(
                visible[:, None, :], jnp.exp(scores - log_total[:, :, None]), 0.0
            )
            grad_prob = jnp.dot(d_o_rows, lat_block, preferred_element_type=jnp.float32).reshape(
                tok_local, heads_here, -1
            )
            grad_score = (
                (probabilities * (grad_prob - row_delta[:, :, None]) * score_scale)
                .astype(jnp.bfloat16)
                .reshape(row_count, -1)
            )
            rounded = probabilities.astype(jnp.bfloat16).reshape(row_count, -1)
            grad_abs = grad_abs + contract_last(grad_score, lat_block)
            grad_rope = grad_rope + contract_last(grad_score, rope_block)
            lat_term = contract_first(query_rows, grad_score) + contract_first(d_o_rows, rounded)
            rope_term = contract_first(rope_rows, grad_score)
            old_lat = lax.dynamic_slice_in_dim(grad_lat, first_key, span_len, 1)
            old_rope = lax.dynamic_slice_in_dim(grad_kr, first_key, span_len, 1)
            grad_lat = lax.dynamic_update_slice_in_dim(grad_lat, old_lat + lat_term, first_key, 1)
            grad_kr = lax.dynamic_update_slice_in_dim(grad_kr, old_rope + rope_term, first_key, 1)
            return (grad_abs, grad_rope, grad_lat, grad_kr)

        return lax.cond(jnp.any(visible), backward_compute, unchanged, state_now)

    backward_init = (
        jnp.zeros((row_count, LATENT), jnp.float32),
        jnp.zeros((row_count, ROPE), jnp.float32),
        jnp.zeros((LATENT, total_tokens), jnp.float32),
        jnp.zeros((ROPE, total_tokens), jnp.float32),
    )
    backward_state = sweep_blocks(backward_step, backward_init, key_parts, 0)
    grad_abs, grad_rope, grad_lat, grad_kr = backward_state
    d_q_abs3 = grad_abs.astype(jnp.bfloat16).reshape(tok_local, heads_here, LATENT)
    d_q_rope = grad_rope.astype(jnp.bfloat16).reshape(tok_local, heads_here * ROPE)
    nope_grad = jnp.einsum("thl,lhn->thn", d_q_abs3, uk_full, preferred_element_type=jnp.float32)
    d_q_nope = nope_grad.astype(jnp.bfloat16).reshape(tok_local, heads_here * NOPE)
    grad_uk = jnp.einsum(
        "thl,thn->lhn", d_q_abs3, nope3, preferred_element_type=jnp.float32
    ).reshape(LATENT // lax.axis_size("seq") * lax.axis_size("seq"), -1)
    grad_uv = jnp.einsum("thl,thv->lhv", o_lat3, grad3, preferred_element_type=jnp.float32).reshape(
        LATENT // lax.axis_size("seq") * lax.axis_size("seq"), -1
    )
    grad_panels = lax.psum_scatter(
        jnp.concatenate([grad_uk, grad_uv], axis=1).astype(jnp.bfloat16),
        "seq",
        scatter_dimension=0,
        tiled=True,
    ).astype(jnp.float32)
    d_w_uk = grad_panels[:, : heads_here * NOPE]
    d_w_uv = grad_panels[:, heads_here * NOPE :]
    partial_shares = (
        lax.psum_scatter(
            grad_lat.astype(jnp.bfloat16), "seq", scatter_dimension=1, tiled=True
        ).astype(jnp.float32),
        lax.psum_scatter(
            grad_kr.astype(jnp.bfloat16), "seq", scatter_dimension=1, tiled=True
        ).astype(jnp.float32),
    )
    key_shares = (
        lax.psum(partial_shares[0].astype(jnp.bfloat16), "fsdp").astype(jnp.float32),
        lax.psum(partial_shares[1].astype(jnp.bfloat16), "fsdp").astype(jnp.float32),
    )
    d_latent_t = key_shares[0].astype(jnp.bfloat16)
    d_k_rope_t = key_shares[1].astype(jnp.bfloat16)
    return (attn_out, d_q_nope, d_q_rope, d_latent_t, d_k_rope_t, d_w_uk, d_w_uv)


def solution(mesh):
    placed = (
        P("seq", "fsdp"),
        P("seq", "fsdp"),
        P(None, "seq"),
        P(None, "seq"),
        P("seq", "fsdp"),
        P("seq", "fsdp"),
        P("seq", "fsdp"),
        P(),
        P(),
    )
    return jax.shard_map(
        on_device,
        mesh=mesh,
        in_specs=placed,
        out_specs=(
            P("seq", "fsdp"),
            P("seq", "fsdp"),
            P("seq", "fsdp"),
            P(None, "seq"),
            P(None, "seq"),
            P("seq", "fsdp"),
            P("seq", "fsdp"),
        ),
        check_vma=False,
    )
```

profile of v0, /device:TPU:0, one launch (start us, length us, event | category | flops | bytes accessed | tf_op | source)
XLA Modules:
  0.0 803.4 jit_solution(9117249375685450106)
XLA Ops:
  9.5 21.2 %all_gather.14 = bf16[64,2048]{1,0:T(8,128)(2,1)S(1)} all-gather(bf16[64,128]{1,0:T(8,128)(2,1)} %param.38), channel_id=1, replica_groups=mesh['seq'=16,'fsdp'=8] {'seq'}, dimensions={1}, use_global_device_ids=true | all-gather | bytes 278528 | tf_op jit(solution)/shard_map/all_gather | solution.py:111
  35.2 11.2 %all-gather.6.cloned.1.call-done = bf16[512,2048]{1,0:T(8,128)(2,1)} async-done(((bf16[32,2048]{1,0:T(8,128)(2,1)}), bf16[512,2048]{1,0:T(8,128)(2,1)}) %all-gather.6.cloned.1.call-update) | async-done | bytes 2097168 | tf_op jit(solution)/shard_map/all_gather | solution.py:75
  52.6 32.6 %all-gather.4.cloned.1.call-done = bf16[512,2048]{1,0:T(8,128)(2,1)} async-done(((bf16[512,128]{1,0:T(8,128)(2,1)}), bf16[512,2048]{1,0:T(8,128)(2,1)}) %all-gather.4.cloned.1.call-update) | async-done | bytes 2097168 | tf_op jit(solution)/shard_map/all_gather | solution.py:110
  85.2 60.8 %while.68 = (s32[]{:T(128)}, f32[128,16]{1,0:T(8,128)S(1)}, f32[128,16]{1,0:T(8,128)S(1)}, s32[128]{0:T(128)S(1)}, s32[2048]{0:T(1024)}, /*index=5*/s32[1,16]{1,...) while((s32[]{:T(128)}, f32[128,16]{1,0:T(8,128)S(1)}, ...), condition=%wide.region_6.8_spmd.clone, body=%wide.region_0.7_spmd.clone.sunk | while | flops 303911200 | bytes 8467486 | solution.py:41
  88.7 5.4 conditional.9
  148.6 64.0 %while.69 = (s32[]{:T(128)}, f32[2048,512]{1,0:T(8,128)}, s32[128]{0:T(128)S(1)}, s32[2048]{0:T(1024)}, s32[1,16]{1,0:T(1,128)S(1)}, /*index=5*/bf16[512,2048]{1...) while((s32[]{:T(128)}, f32[2048,512]{1,0:T(8,128)}, ...), condition=%wide.region_11.13_spmd.clone, body=%wide.region_7.12_spmd.clone.sunk | while | flops 572866816 | bytes 14497786 | solution.py:41
  152.0 8.8 %conditional.10 = (f32[2048,512]{1,0:T(8,128)}) conditional(s32[]{:T(128)} %convert_element_type.143, f32[2048,512]{1,0:T(8,128)} %get-tuple-element.2147, (pred[128,128]{1,0:T(8,128)(4,1)S(1)}, bf16[512,2048]{1,0:T(8,128)(2,1)}, s32[]{:T(128)}, bf16[2048,512]{1,0:T(8,128)(2,1)S(1)}, bf16[64,2048]{1,0:T(8,128)(2,1)S(1)}, ...), branch_computations={%region_9.10_spmd, %region_10.11_spmd} | conditional | flops 572784640 | bytes 14476808 | solution.py:127
  155.2 5.5 convolution_add_fusion.1
  212.6 3.9 convert_element_type.110
  216.5 4.0 copy.88
  220.5 6.3 multiply_reduce_fusion
  226.9 4.1 copy.92
  236.9 70.4 %while.70 = (s32[]{:T(128)}, f32[2048,512]{1,0:T(8,128)}, f32[2048,64]{0,1:T(8,128)S(1)}, f32[512,2048]{0,1:T(8,128)}, f32[64,2048]{1,0:T(8,128)}, /*index=5*/s3...) while((s32[]{:T(128)}, f32[2048,512]{1,0:T(8,128)}, ...), condition=%wide.region_17.19_spmd.clone, body=%wide.region_13.18_spmd.clone.sunk | while | flops 1446600960 | bytes 70835472 | solution.py:41
  240.3 15.1 %conditional.11 = ((f32[2048,512]{1,0:T(8,128)}, f32[2048,64]{0,1:T(8,128)S(1)}, f32[512,2048]{0,1:T(8,128)}, f32[64,2048]{1,0:T(8,128)})) conditional(s32[]{:T(128)} %convert_element_type.144, (f32[2048,512]{1,0:T(8,128)}, f32[2048,64]{0,1:T(8,128)S(1)}, f32[512,2048]{0,1:T(8,128)}, f32[64,2048]{1,0:T(8,128)}) %tuple.258, ...), branch_computations={%region_15.16_spmd, %region_16.17_spmd} | conditional | flops 1446518784 | bytes 70814376 | solution.py:170
  317.1 3.9 convolution_convert_fusion
  321.0 3.9 copy.103
  327.5 3.9 convolution_convert_fusion.1
  331.5 4.0 copy.102
  335.4 4.7 pad_maximum_fusion
  350.0 223.0 %reduce-scatter.12.cloned.1.call-done = bf16[128,64]{1,0:T(8,128)(2,1)} async-done(((bf16[2048,64]{1,0:T(8,128)(2,1)}), bf16[128,64]{1,0:T(8,128)(2,1)}) %reduce-scatter.12.cloned.1.call-update) | async-done | bytes 16400
  573.8 42.2 %psum.15 = bf16[64,128]{1,0:T(8,128)(2,1)} all-reduce(bf16[64,128]{1,0:T(8,128)(2,1)S(1)} %copy.111), channel_id=1, replica_groups=mesh['seq'=16,'fsdp'=8] {'fsdp'}, use_global_device_ids=true, to_apply=%region_21.23 | all-reduce | flops 8192 | bytes 32768 | tf_op jit(solution)/shard_map/psum | solution.py:208
  616.0 22.2 %reduce-scatter.10.cloned.1.call-done = bf16[128,512]{1,0:T(8,128)(2,1)} async-done(((bf16[2048,512]{1,0:T(8,128)(2,1)}), bf16[128,512]{1,0:T(8,128)(2,1)}) %reduce-scatter.10.cloned.1.call-update) | async-done | bytes 131088
  639.9 69.0 %reduce-scatter.8.cloned.1.call-done = bf16[32,4096]{1,0:T(8,128)(2,1)} async-done(((bf16[512,4096]{1,0:T(8,128)(2,1)}), bf16[32,4096]{1,0:T(8,128)(2,1)}) %reduce-scatter.8.cloned.1.call-update) | async-done | bytes 262160 | tf_op jit(solution)/shard_map/reduce_scatter | solution.py:190
  710.8 84.2 %all-reduce.2.cloned.1.call-done = bf16[512,128]{1,0:T(8,128)(2,1)} async-done(((bf16[512,128]{1,0:T(8,128)(2,1)}), bf16[512,128]{1,0:T(8,128)(2,1)}) %all-reduce.2.cloned.1.call-update) | async-done | bytes 131088 | tf_op jit(solution)/shard_map/psum | solution.py:207
  (342 shorter events, 173.7 us)
Async XLA Ops:
  7.2 28.0 %copy-start = (s32[16,16]{1,0:T(8,128)S(1)}, s32[16,16]{1,0:T(8,128)}, u32[]{:S(2)}) copy-start(s32[16,16]{1,0:T(8,128)} %param.43) | copy-start | bytes 3076
  7.2 26.2 %copy-start.14 = (bf16[128,2048]{1,0:T(8,128)(2,1)S(1)}, bf16[128,2048]{1,0:T(8,128)(2,1)}, u32[]{:S(2)}) copy-start(bf16[128,2048]{1,0:T(8,128)(2,1)} %param.41) | copy-start | bytes 1572868
  7.2 39.2 %all-gather.6.cloned.1.call-start = ((), (), s32[]{:S(2)}) async-start(), calls=%async_computation.4 | async-start | bytes 2228224 | tf_op jit(solution)/shard_map/all_gather | solution.py:75
  7.9 77.3 %all-gather.4.cloned.1.call-start = ((), (), s32[]{:S(2)}) async-start(), calls=%async_computation.3 | async-start | bytes 2228224 | tf_op jit(solution)/shard_map/all_gather | solution.py:110
  8.7 207.8 %all-gather.8.cloned.1.call-start = ((), (), s32[]{:S(2)}) async-start(), calls=%async_computation.5 | async-start | bytes 2228224 | tf_op jit(solution)/shard_map/all_gather | solution.py:76
  9.4 563.6 %reduce-scatter.12.cloned.1.call-start = ((), (), s32[]{:S(2)}) async-start(), calls=%async_computation.9 | async-start | bytes 557056
  33.4 15.9 %copy-start.9 = (bf16[128,2048]{0,1:T(8,128)(2,1)}, bf16[128,2048]{0,1:T(8,128)(2,1)S(1)}, u32[]{:S(2)}) copy-start(bf16[128,2048]{0,1:T(8,128)(2,1)S(1)} %copy.112) | copy-start | bytes 1572868
  49.2 1.4 copy-start.8
  212.6 3.9 copy-start.13
  216.5 4.0 copy-start.11
  242.6 1.6 copy-start.2
  248.2 3.4 copy-start.3
  253.4 1.9 copy-start.4
  309.4 328.8 %reduce-scatter.10.cloned.1.call-start = ((), (), s32[]{:S(2)}) async-start(), calls=%async_computation.8 | async-start | bytes 2228224
  312.9 2.6 copy-start.12
  315.5 1.6 copy-start.5
  315.5 393.5 %reduce-scatter.8.cloned.1.call-start = ((), (), s32[]{:S(2)}) async-start(), calls=%async_computation.7 | async-start | bytes 4456448 | tf_op jit(solution)/shard_map/reduce_scatter | solution.py:190
  325.0 2.5 copy-start.10
  327.5 4.0 copy-start.6
  340.1 454.9 %all-reduce.2.cloned.1.call-start = ((), (), s32[]{:S(2)}) async-start(), calls=%async_computation.6 | async-start | bytes 262144 | tf_op jit(solution)/shard_map/psum | solution.py:207
  343.5 2.4 copy-start.7
  345.9 450.7 %copy-start.1 = (s32[16,16]{1,0:T(8,128)S(1)}, s32[16,16]{1,0:T(8,128)}, u32[]{:S(2)}) copy-start(s32[16,16]{1,0:T(8,128)} %param.43) | copy-start | bytes 3076
Sparse Core Ops, SparseCore 0:
  9.7 36.5 all-gather.5
  48.0 37.1 all-gather.3
  86.9 34.2 all-gather.7
  309.6 263.3 reduce-scatter.11
  575.3 62.8 reduce-scatter.9
  640.6 68.2 reduce-scatter.7
  712.1 82.8 all-reduce.1
where the time goes:
time: 794 us; the launch traced here: 803 us
  waiting for transfers between devices  444 us (56%)
  local copies, waits for them, and re-layouts  121 us (15%)
  loops' own time  65.9 us (8%)
  blocking collectives  63.5 us (8%)
  other arithmetic  49.2 us (6%)
  matrix products  44.7 us (6%)
  between operations  14.4 us (2%)
    unnamed x9, waiting for transfers between devices  247 us
    psum x1, waiting for transfers between devices, on_device(): lax.psum(partial_shares[0].astype(jnp.bfloat16), 'fsdp').astype(jnp.float32)  84.2 us
    reduce_scatter x1, waiting for transfers between devices, on_device(): lax.psum_scatter(jnp.concatenate([grad_uk, grad_uv], axis=1).astype(jnp.b...  69 us
    another operation x3, loops' own time, sweep_blocks(): return lax.fori_loop(0, key_count // span_len, visit_block, state_now)  65.2 us
    psum x1, blocking collectives, on_device(): lax.psum(partial_shares[1].astype(jnp.bfloat16), 'fsdp').astype(jnp.float32)  42.2 us
    dynamic_slice x48, local copies, waits for them, and re-layouts, visibility(): key_seg = lax.dynamic_slice_in_dim(seg_ids, first_key, span_len)  36.8 us
    all_gather x1, waiting for transfers between devices, on_device(): lax.all_gather(latent_t, 'seq', axis=1, tiled=True)  32.6 us
    dynamic_slice x48, local copies, waits for them, and re-layouts, visibility(): block_col = lax.dynamic_slice_in_dim(flag_rows, first_key // BLOCK, 1, 1)  28.1 us
  transfers between devices with their start and end apart: 7, of which 6 were waited for; matrix products, arithmetic and copies ran while one was open for 17% of the time, Pallas kernels for 0%

commit v1 on v0

v1 whole, which is shorter than its diff:
```python
import functools
import math

import jax
import jax.numpy as jnp
from jax import lax
from jax.experimental import pallas as pl
from jax.experimental.pallas import tpu as pltpu
from jax.sharding import PartitionSpec as P

F32, BF16 = jnp.float32, jnp.bfloat16
MESH = pl.DeviceIdType.MESH
NEG = -1e30
SCALE = 1.0 / math.sqrt(192.0)
SCALE_LOG2E = SCALE * math.log2(math.e)
TILES = 8
PART = 144

SEQ_PEERS = [
    (dy, dx, dc) for dy in (1, 3, 0, 2) for dx in (0, 1) for dc in (0, 1) if (dy, dx, dc) != (0, 0, 0)
]
CHIP_PEERS = [(0, 1), (1, 0), (3, 0), (1, 1), (3, 1), (2, 0), (2, 1)]


def dot(left, right):
    return lax.dot_general(left, right, (((1,), (0,)), ((), ())), preferred_element_type=F32)


def unpack_rope(x):
    return jnp.concatenate([x[:, :64], x[:, 64:]], axis=0)


def pack_rope(x):
    return jnp.concatenate([x[:64], x[64:]], axis=1)


def tile_of(lat, t, lo, hi):
    return jnp.concatenate([lat[0, t, lo:hi, :], lat[1, t, lo:hi, :]], axis=1)


def fused(
    seg, anc, qn_in, qr_in, lt_in, kr_in, uk_in, uv_in, g_in,
    ro, rw, fin,
    lat, sw, iw, sq, iq, wt, wtT, kcT, vT, kc, v, sc, dk, dv, so, dl, ra, sa, rb, sb, rc, dws,
    l1s, l1r, l2s, l2r, l3s, l3r, iws, iwr, iqs, iqr, os, orr, ras, rar, rbs, rbr, rcs, rcr, ws, wr, es, er,
):
    s, f = lax.axis_index("seq"), lax.axis_index("fsdp")
    y, x, c = s // 4, (s // 2) % 2, s % 2
    k = s // 2
    h, z = f // 4, f % 4

    def seq_peer(rel):
        return ((y + rel[0]) % 4) * 4 + ((x + rel[1]) % 2) * 2 + (c + rel[2]) % 2

    def chip_peer(rel):
        return ((y + rel[0]) % 4) * 2 + (x + rel[1]) % 2

    def z_peer(dz):
        return (z + dz) % 4

    other_core = (k * 2 + 1 - c, f)
    zrow = pl.multiple_of(z * PART, 16)

    def remote(src, dst, ssem, rsem, device):
        return pltpu.make_async_remote_copy(
            src_ref=src, dst_ref=dst, send_sem=ssem, recv_sem=rsem, device_id=device, device_id_type=MESH
        )

    bar = pltpu.get_barrier_semaphore()
    peers = [(seq_peer(r), f) for r in SEQ_PEERS]
    peers += [(s, h * 4 + z_peer(dz)) for dz in (1, 2, 3)]
    peers += [(chip_peer(r) * 2 + c, (1 - h) * 4 + z) for r in [(0, 0)] + CHIP_PEERS]
    for p in peers:
        pl.semaphore_signal(bar, inc=1, device_id=p, device_id_type=MESH)

    lat[c, k, 0:512, :] = lt_in[...]
    lat[c, k, 512:576, :] = kr_in[...]
    for d in range(16):
        sw[d, 0:32, :] = uk_in[:, 128 * d : 128 * d + 128]
        sw[d, 32:64, :] = uv_in[:, 128 * d : 128 * d + 128]
        sq[d, 0:128, :] = qn_in[:, 128 * d : 128 * d + 128]
        sq[d, 128:256, :] = g_in[:, 128 * d : 128 * d + 128]
    for pair in range(8):
        both = qr_in[:, 128 * pair : 128 * pair + 128].astype(F32)
        sq[2 * pair, 256:320, :] = pack_rope(both[:, :64]).astype(BF16)
        sq[2 * pair + 1, 256:320, :] = pack_rope(both[:, 64:]).astype(BF16)
    iw[s] = sw[s]
    iq[s] = sq[s]
    pl.semaphore_wait(bar, len(peers))

    sends = []

    for i, r in enumerate(CHIP_PEERS):
        cp = remote(
            lat.at[c, k, pl.ds(zrow, PART)], lat.at[c, k, pl.ds(zrow, PART)],
            l1s.at[i], l1r.at[k], (chip_peer(r) * 2 + c, f),
        )
        cp.start()
        sends.append(cp)
    cp = remote(lat.at[c, k], lat.at[c, k], l3s.at[k], l3r.at[k], other_core)
    cp.start()
    sends.append(cp)
    for i, r in enumerate(SEQ_PEERS):
        p = seq_peer(r)
        cp = remote(sw.at[p], iw.at[s], iws.at[i], iwr.at[s], (p, f))
        cp.start()
        sends.append(cp)
    for i, r in enumerate(SEQ_PEERS):
        p = seq_peer(r)
        cp = remote(sq.at[p], iq.at[s], iqs.at[i], iqr.at[s], (p, f))
        cp.start()
        sends.append(cp)
    for i, r in enumerate(CHIP_PEERS):
        q = chip_peer(r)
        piece = lat.at[c, q, pl.ds(zrow, PART)]
        remote(piece, piece, l1s.at[i], l1r.at[q], other_core).wait_recv()
        for j, dz in enumerate((1, 3, 2)):
            cp = remote(piece, piece, l2s.at[3 * i + j], l2r.at[4 * q + z], (s, h * 4 + z_peer(dz)))
            cp.start()
            sends.append(cp)
    for i, r in enumerate(CHIP_PEERS):
        q = chip_peer(r)
        for dz in (1, 3, 2):
            zz = z_peer(dz)
            piece = lat.at[c, q, pl.ds(pl.multiple_of(zz * PART, 16), PART)]
            remote(piece, piece, l2s.at[0], l2r.at[4 * q + zz], other_core).wait_recv()
        cp = remote(lat.at[c, q], lat.at[c, q], l3s.at[q], l3r.at[q], other_core)
        cp.start()
        sends.append(cp)

    for r in SEQ_PEERS:
        p = seq_peer(r)
        remote(iw.at[p], iw.at[p], iws.at[0], iwr.at[p], other_core).wait_recv()
    for d in range(16):
        wt[0, 32 * d : 32 * d + 32, :] = iw[d, 0:32, :]
        wt[1, 32 * d : 32 * d + 32, :] = iw[d, 32:64, :]
    wtT[0:128, :] = wt[0].astype(F32).T.astype(BF16)
    wtT[128:256, :] = wt[1].astype(F32).T.astype(BF16)
    for r in [(0, 0)] + CHIP_PEERS:
        q = chip_peer(r)
        block = lat.at[1 - c, q]
        remote(block, block, l3s.at[0], l3r.at[q], other_core).wait_recv()

    for t in range(TILES):
        rope = tile_of(lat, t, 512, 576)
        kv = dot(wtT[...], tile_of(lat, t, 0, 512))
        kcT[t, 0:128, :] = kv[:128].astype(BF16)
        kcT[t, 128:192, :] = rope
        vT[t] = kv[128:].astype(BF16)
        kc[t, :, 0:128] = kv[:128].T.astype(BF16)
        kc[t, :, 128:192] = rope.astype(F32).T.astype(BF16)
        v[t] = kv[128:].T.astype(BF16)

    lane = lax.broadcasted_iota(jnp.int32, (1, 256), 1)

    def bias_of(a, b):
        seen = (seg[128 * a] == seg[128 * b]) | (anc[a, b] == 1)
        return jnp.where(seen, 0.0, NEG).astype(F32)

    def attend(I):
        a0, a1 = iq[2 * I], iq[2 * I + 1]
        qn = jnp.concatenate([a0[0:128], a1[0:128]], axis=0)
        g = jnp.concatenate([a0[128:256], a1[128:256]], axis=0)
        qr = jnp.concatenate(
            [unpack_rope(a0[256:320].astype(F32)), unpack_rope(a1[256:320].astype(F32))], axis=0
        )
        qT = jnp.concatenate([qn.astype(F32).T, qr.T], axis=0).astype(BF16)
        qc = jnp.concatenate([qn, qr.astype(BF16)], axis=1)
        gT32 = g.astype(F32).T
        gT = gT32.astype(BF16)
        top = jnp.full((1, 256), NEG, F32)
        for J in range(I + 1):
            scores = dot(kc[J], qT)
            if J < I:
                halves = []
                for b in range(2):
                    bias = jnp.where(
                        lane < 128, bias_of(2 * I, 2 * J + b), bias_of(2 * I + 1, 2 * J + b)
                    )
                    halves.append(scores[128 * b : 128 * b + 128] + bias)
                scores = jnp.concatenate(halves, axis=0)
            else:
                key = lax.broadcasted_iota(jnp.int32, (256, 256), 0)
                query = lax.broadcasted_iota(jnp.int32, (256, 256), 1)
                bias = jnp.where(lane < 128, 0.0, bias_of(2 * I + 1, 2 * I))
                scores = jnp.concatenate([scores[:128] + bias, scores[128:]], axis=0)
                scores = jnp.where(key <= query, scores, NEG)
            sc[J] = scores
            top = jnp.maximum(top, jnp.max(scores, axis=0, keepdims=True))
        top = top * SCALE_LOG2E
        total = jnp.zeros((1, 256), F32)
        oT = jnp.zeros((128, 256), F32)
        for J in range(I + 1):
            weight = jnp.exp2(sc[J] * SCALE_LOG2E - top)
            total = total + jnp.sum(weight, axis=0, keepdims=True)
            sc[J] = weight
            oT = oT + dot(vT[J], weight.astype(BF16))
        inverse = 1.0 / total
        oT = oT * inverse
        delta = jnp.sum(oT * gT32, axis=0, keepdims=True)
        dqT = jnp.zeros((192, 256), F32)
        for J in range(I + 1):
            prob = sc[J] * inverse
            ds = (prob * (dot(v[J], gT) - delta)).astype(BF16)
            dqT = dqT + dot(kcT[J], ds)
            dk_now = dot(ds, qc)
            dv_now = dot(prob.astype(BF16), g)
            if I == TILES - 1:
                dk[J] = dk_now
                dv[J] = dv_now
            else:
                dk[J] += dk_now
                dv[J] += dv_now
        o = oT.T.astype(BF16)
        dqT = dqT * SCALE
        dqn = dqT[:128].T.astype(BF16)
        dqr = dqT[128:].T
        for e in range(2):
            lo = 128 * e
            so[2 * I + e, 0:128, :] = o[lo : lo + 128]
            so[2 * I + e, 128:256, :] = dqn[lo : lo + 128]
            so[2 * I + e, 256:320, :] = pack_rope(dqr[lo : lo + 128]).astype(BF16)

    def send_out(I):
        for e in range(2):
            d = 2 * I + e

            @pl.when(s != d)
            def _():
                remote(so.at[d], ro.at[s], os.at[d], orr.at[s], (d, f)).start()

            @pl.when(s == d)
            def _():
                ro[s] = so[d]

    def key_grads(I, w_grad):
        dkt = dk[I] * SCALE
        kv = jnp.concatenate([dkt[:, :128], dv[I]], axis=1)
        w = jnp.concatenate([wt[0], wt[1]], axis=1)
        lat_grad = dot(w, kv.T.astype(BF16)).astype(BF16)
        rope_grad = dkt[:, 128:].T.astype(BF16)
        for e in range(2):
            dl[e, I, 0:512, :] = lat_grad[:, 128 * e : 128 * e + 128]
            dl[e, I, 512:576, :] = rope_grad[:, 128 * e : 128 * e + 128]
        remote(dl.at[1 - c, I], ra.at[I], ras.at[I], rar.at[I], other_core).start()
        return w_grad + dot(tile_of(lat, I, 0, 512), kv.astype(BF16))

    def stage_b(I):
        remote(ra.at[I], ra.at[I], ras.at[I], rar.at[I], other_core).wait_recv()
        sa[I] = (dl[c, I].astype(F32) + ra[I].astype(F32)).astype(BF16)
        for j, dz in enumerate((1, 3, 2)):
            zz = z_peer(dz)
            remote(
                sa.at[I, pl.ds(pl.multiple_of(zz * PART, 16), PART)], rb.at[I, z],
                rbs.at[3 * I + j], rbr.at[4 * I + z], (s, h * 4 + zz),
            ).start()

    def stage_c(I):
        acc = sa[I, pl.ds(zrow, PART), :].astype(F32)
        for dz in (1, 3, 2):
            zz = z_peer(dz)
            remote(rb.at[I, zz], rb.at[I, zz], rbs.at[3 * I], rbr.at[4 * I + zz], other_core).wait_recv()
            acc = acc + rb[I, zz].astype(F32)
        sb[I] = acc.astype(BF16)
        dest = 2 * I + c
        slot = h * 8 + k

        @pl.when(k != I)
        def _():
            remote(sb.at[I], rc.at[slot], rcs.at[2 * I], rcr.at[slot], (dest, f)).start()

        @pl.when(k == I)
        def _():
            rc[slot] = sb[I]

        remote(sb.at[I], rc.at[slot], rcs.at[2 * I + 1], rcr.at[slot], (dest, (1 - h) * 4 + z)).start()

    w_grad = jnp.zeros((512, 256), F32)
    for I in reversed(range(TILES)):
        for e in range(2):
            d = 2 * I + e

            @pl.when(s != d)
            def _():
                remote(iq.at[d], iq.at[d], iqs.at[0], iqr.at[d], other_core).wait_recv()

        attend(I)
        w_grad = key_grads(I, w_grad)
        send_out(I)
        if I + 1 < TILES:
            stage_b(I + 1)
        if I + 2 < TILES:
            stage_c(I + 2)
    stage_c(1)
    stage_b(0)
    w_grad = w_grad.astype(BF16)
    for d in range(16):
        dws[d, 0:32, :] = w_grad[32 * d : 32 * d + 32, :128]
        dws[d, 32:64, :] = w_grad[32 * d : 32 * d + 32, 128:]
    for i, r in enumerate(SEQ_PEERS):
        p = seq_peer(r)
        cp = remote(dws.at[p], rw.at[s], ws.at[i], wr.at[s], (p, f))
        cp.start()
        sends.append(cp)
    rw[s] = dws[s]
    stage_c(0)

    acc = rc[h * 8 + k].astype(F32)
    for hh in (h, 1 - h):
        for r in [(0, 0)] + CHIP_PEERS:
            slot = hh * 8 + chip_peer(r)
            if hh is h and r == (0, 0):
                continue
            remote(rc.at[slot], rc.at[slot], rcs.at[0], rcr.at[slot], other_core).wait_recv()
            acc = acc + rc[slot].astype(F32)
    fin[pl.ds(zrow, PART), :] = acc.astype(BF16)
    for j, dz in enumerate((1, 3, 2)):
        piece = fin.at[pl.ds(zrow, PART)]
        cp = remote(piece, piece, es.at[j], er.at[z], (s, h * 4 + z_peer(dz)))
        cp.start()
        sends.append(cp)

    for r in SEQ_PEERS:
        p = seq_peer(r)
        remote(ro.at[p], ro.at[p], os.at[0], orr.at[p], other_core).wait_recv()
        remote(rw.at[p], rw.at[p], ws.at[0], wr.at[p], other_core).wait_recv()
    for dz in (1, 3, 2):
        zz = z_peer(dz)
        piece = fin.at[pl.ds(pl.multiple_of(zz * PART, 16), PART)]
        remote(piece, piece, es.at[0], er.at[zz], other_core).wait_recv()
    for cp in sends:
        cp.wait_send()
    for I in range(TILES):
        remote(ra.at[I], ra.at[I], ras.at[I], rar.at[I], other_core).wait_send()
        for j in range(3):
            remote(rb.at[I, 0], rb.at[I, 0], rbs.at[3 * I + j], rbr.at[0], other_core).wait_send()

        @pl.when(k != I)
        def _():
            remote(sb.at[I], sb.at[I], rcs.at[2 * I], rcr.at[0], other_core).wait_send()

        remote(sb.at[I], sb.at[I], rcs.at[2 * I + 1], rcr.at[0], other_core).wait_send()
        for e in range(2):
            d = 2 * I + e

            @pl.when(s != d)
            def _():
                remote(so.at[d], so.at[d], os.at[d], orr.at[0], other_core).wait_send()


def unpack(ro, rw, fin, out, dqn, dqr, dlat, dkr, duk, duv):
    for d in range(16):
        cols = slice(128 * d, 128 * d + 128)
        out[:, cols] = ro[d, 0:128, :]
        dqn[:, cols] = ro[d, 128:256, :]
        duk[:, cols] = rw[d, 0:32, :].astype(F32)
        duv[:, cols] = rw[d, 32:64, :].astype(F32)
    for pair in range(8):
        both = [unpack_rope(ro[2 * pair + e, 256:320, :].astype(F32)) for e in range(2)]
        dqr[:, 128 * pair : 128 * pair + 128] = jnp.concatenate(both, axis=1).astype(BF16)
    dlat[...] = fin[0:512, :]
    dkr[...] = fin[512:576, :]


def on_device(q_nope, q_rope, latent_t, k_rope_t, w_uk, w_uv, grad_out, seg_ids, anc_flags):
    vmem = pl.BlockSpec(memory_space=pltpu.VMEM)
    smem = pl.BlockSpec(memory_space=pltpu.SMEM)
    dma = pltpu.SemaphoreType.DMA
    sem_counts = [7, 8, 21, 32, 8, 8, 15, 16, 15, 16, 16, 16, 8, 8, 24, 32, 16, 16, 15, 16, 3, 4]
    parts = pl.pallas_call(
        fused,
        out_shape=[
            jax.ShapeDtypeStruct((16, 320, 128), BF16),
            jax.ShapeDtypeStruct((16, 64, 128), BF16),
            jax.ShapeDtypeStruct((576, 128), BF16),
        ],
        in_specs=[smem, smem] + [vmem] * 7,
        out_specs=[vmem] * 3,
        scratch_shapes=[
            pltpu.VMEM((2, 8, 576, 128), BF16),
            pltpu.VMEM((16, 64, 128), BF16),
            pltpu.VMEM((16, 64, 128), BF16),
            pltpu.VMEM((16, 320, 128), BF16),
            pltpu.VMEM((16, 320, 128), BF16),
            pltpu.VMEM((2, 512, 128), BF16),
            pltpu.VMEM((256, 512), BF16),
            pltpu.VMEM((8, 192, 256), BF16),
            pltpu.VMEM((8, 128, 256), BF16),
            pltpu.VMEM((8, 256, 192), BF16),
            pltpu.VMEM((8, 256, 128), BF16),
            pltpu.VMEM((8, 256, 256), F32),
            pltpu.VMEM((8, 256, 192), F32),
            pltpu.VMEM((8, 256, 128), F32),
            pltpu.VMEM((16, 320, 128), BF16),
            pltpu.VMEM((2, 8, 576, 128), BF16),
            pltpu.VMEM((8, 576, 128), BF16),
            pltpu.VMEM((8, 576, 128), BF16),
            pltpu.VMEM((8, 4, PART, 128), BF16),
            pltpu.VMEM((8, PART, 128), BF16),
            pltpu.VMEM((16, PART, 128), BF16),
            pltpu.VMEM((16, 64, 128), BF16),
        ]
        + [dma((n,)) for n in sem_counts],
        compiler_params=pltpu.CompilerParams(
            collective_id=0, has_side_effects=True, vmem_limit_bytes=56 * 1024 * 1024
        ),
        name="attention_exchange",
    )(seg_ids, anc_flags, q_nope, q_rope, latent_t, k_rope_t, w_uk, w_uv, grad_out)
    bf, fl = BF16, F32
    return pl.pallas_call(
        unpack,
        out_shape=[
            jax.ShapeDtypeStruct((128, 2048), bf),
            jax.ShapeDtypeStruct((128, 2048), bf),
            jax.ShapeDtypeStruct((128, 1024), bf),
            jax.ShapeDtypeStruct((512, 128), bf),
            jax.ShapeDtypeStruct((64, 128), bf),
            jax.ShapeDtypeStruct((32, 2048), fl),
            jax.ShapeDtypeStruct((32, 2048), fl),
        ],
        in_specs=[vmem] * 3,
        out_specs=[vmem] * 7,
        compiler_params=pltpu.CompilerParams(vmem_limit_bytes=32 * 1024 * 1024),
        name="unpack",
    )(*parts)


def solution(mesh):
    placed = (
        P("seq", "fsdp"),
        P("seq", "fsdp"),
        P(None, "seq"),
        P(None, "seq"),
        P("seq", "fsdp"),
        P("seq", "fsdp"),
        P("seq", "fsdp"),
        P(),
        P(),
    )
    return jax.shard_map(
        on_device,
        mesh=mesh,
        in_specs=placed,
        out_specs=(
            P("seq", "fsdp"),
            P("seq", "fsdp"),
            P("seq", "fsdp"),
            P(None, "seq"),
            P(None, "seq"),
            P("seq", "fsdp"),
            P("seq", "fsdp"),
        ),
        check_vma=False,
    )
```

time: 794 us -> 89.9 us (0.11); the launches traced: 803 us -> 89.6 us
  waiting for transfers between devices: 444 us -> 0 us
  local copies, waits for them, and re-layouts: 121 us -> 3.17 us
  Pallas kernels: 0 us -> 85.8 us
  loops' own time: 65.9 us -> 0 us
  blocking collectives: 63.5 us -> 0 us
  other arithmetic: 49.2 us -> 0 us
  matrix products: 44.7 us -> 0 us
  between operations: 14.4 us -> 0.65 us
    unnamed x9 -> x0, waiting for transfers between devices: 247 us -> none
    pallas_call x0 -> x2, Pallas kernels: none -> 85.8 us  [the longest x1 84.2 us: on_device(): pl.pallas_call(fused, out_shape=[jax.ShapeDtypeStruct((16, 320, 128), BF1...]
    psum x1 -> x0, waiting for transfers between devices: 84.2 us -> none  [on_device(): lax.psum(partial_shares[0].astype(jnp.bfloat16), 'fsdp').astype(jnp.float32)]
    reduce_scatter x1 -> x0, waiting for transfers between devices: 69 us -> none  [on_device(): lax.psum_scatter(jnp.concatenate([grad_uk, grad_uv], axis=1).astype(jnp.b...]
    another operation x51 -> x0, loops' own time: 65.9 us -> none  [the longest x3 65.2 us: sweep_blocks(): return lax.fori_loop(0, key_count // span_len, visit_block, state_now)]
    dynamic_slice x98 -> x0, local copies, waits for them, and re-layouts: 65.6 us -> none  [the longest x48 36.8 us: visibility(): key_seg = lax.dynamic_slice_in_dim(seg_ids, first_key, span_len)]
    dot_general x18 -> x0, matrix products: 44.7 us -> none  [the longest x3 8.42 us: contract_last(): lax.dot_general(left, right, (((1,), (1,)), ((), ())), preferred_element_...]
    all_gather x3 -> x0, waiting for transfers between devices: 43.8 us -> none  [the longest x1 32.6 us: on_device(): lax.all_gather(latent_t, 'seq', axis=1, tiled=True)]
  transfers between devices with their start and end apart: 7 -> 0, of which waited for: 6 -> 0; matrix products, arithmetic and copies ran while one was open for 17% -> 0% of each run, Pallas kernels for 0% -> 0%
where the time goes in v1:
time: 89.9 us; the launch traced here: 89.6 us
  Pallas kernels  85.8 us (95%)
  local copies, waits for them, and re-layouts  3.17 us (4%)
    pallas_call x1, Pallas kernels, on_device(): pl.pallas_call(fused, out_shape=[jax.ShapeDtypeStruct((16, 320, 128), BF1...  84.2 us
    unnamed x6, local copies, waits for them, and re-layouts  3.17 us

profile of v1, /device:TPU:0, one launch (start us, length us, event | category | flops | bytes accessed | tf_op | source)
XLA Modules:
  0.0 89.6 jit_solution(18408452100722017425)
XLA Ops:
  0.6 84.2 %attention_exchange.1 = (bf16[16,320,128]{2,1,0:T(8,128)(2,1)}, bf16[16,64,128]{2,1,0:T(8,128)(2,1)}, bf16[576,128]{1,0:T(8,128)(2,1)}) custom-call(s32[2048]{0:T(1024)} %seg.1, s32[16,16]{1,0:T(8,128)} %anc.1, bf16[128,2048]{1,0:T(8,128)(2,1)} %qn_in.1, bf16[128,1024]{1,0:T(8,128)(2,1)} %qr_in.1, bf16[512,128]{1,0:T(8,128)(2,1)} %lt_in.1, ...), custom_call_target="tpu_custom_call" | custom-call | tf_op jit(solution)/shard_map/attention_exchange/pallas_call | solution.py:370
  84.8 0.0 copy-start
  84.8 1.3 %copy-done = bf16[16,320,128]{2,1,0:T(8,128)(2,1)S(1)} copy-done((bf16[16,320,128]{2,1,0:T(8,128)(2,1)S(1)}, bf16[16,320,128]{2,1,0:T(8,128)(2,1)}, u32[]{:S(2)}) %copy-start) | copy-done | bytes 1310744
  86.2 0.0 copy-start.1
  86.2 0.9 %copy-done.1 = bf16[16,64,128]{2,1,0:T(8,128)(2,1)S(1)} copy-done((bf16[16,64,128]{2,1,0:T(8,128)(2,1)S(1)}, bf16[16,64,128]{2,1,0:T(8,128)(2,1)}, u32[]{:S(2)}) %copy-start.1) | copy-done | bytes 262168
  87.1 0.0 copy-start.2
  87.1 0.9 %copy-done.2 = bf16[576,128]{1,0:T(8,128)(2,1)S(1)} copy-done((bf16[576,128]{1,0:T(8,128)(2,1)S(1)}, bf16[576,128]{1,0:T(8,128)(2,1)}, u32[]{:S(2)}) %copy-start.2) | copy-done | bytes 147480
  88.0 1.6 %unpack.1 = (bf16[128,2048]{1,0:T(8,128)(2,1)}, bf16[128,2048]{1,0:T(8,128)(2,1)}, bf16[128,1024]{1,0:T(8,128)(2,1)}, bf16[512,128]{1,0:T(8,128)(2,1)}, bf16[64,...) custom-call(bf16[16,320,128]{2,1,0:T(8,128)(2,1)S(1)} %copy-done, bf16[16,64,128]{2,1,0:T(8,128)(2,1)S(1)} %copy-done.1, ...), custom_call_target="tpu_custom_call" | custom-call | tf_op jit(solution)/shard_map/unpack/pallas_call | solution.py:410
Async XLA Ops:
  84.8 1.3 %copy-start = (bf16[16,320,128]{2,1,0:T(8,128)(2,1)S(1)}, bf16[16,320,128]{2,1,0:T(8,128)(2,1)}, u32[]{:S(2)}) copy-start(bf16[16,320,128]{2,1,0:T(8,128)(2,1)} %get-tuple-element.10.ro) | copy-start | bytes 3932164
  86.2 0.9 %copy-start.1 = (bf16[16,64,128]{2,1,0:T(8,128)(2,1)S(1)}, bf16[16,64,128]{2,1,0:T(8,128)(2,1)}, u32[]{:S(2)}) copy-start(bf16[16,64,128]{2,1,0:T(8,128)(2,1)} %get-tuple-element.11.rw) | copy-start | bytes 786436
  87.1 0.9 %copy-start.2 = (bf16[576,128]{1,0:T(8,128)(2,1)S(1)}, bf16[576,128]{1,0:T(8,128)(2,1)}, u32[]{:S(2)}) copy-start(bf16[576,128]{1,0:T(8,128)(2,1)} %get-tuple-element.12.fin) | copy-start | bytes 442372

commit v2 on v1

v2 whole, which is shorter than its diff:
```python
import functools
import math

import jax
import jax.numpy as jnp
from jax import lax
from jax.experimental import pallas as pl
from jax.experimental.pallas import tpu as pltpu
from jax.sharding import PartitionSpec as P

F32, BF16 = jnp.float32, jnp.bfloat16
MESH = pl.DeviceIdType.MESH
NEG = -1e30
SCALE = 1.0 / math.sqrt(192.0)
SCALE_LOG2E = SCALE * math.log2(math.e)
TILES = 8
LAG = 2
PART = 144
ALONG_Z = 448
PART_Z = ALONG_Z // 4
REST = 576 - ALONG_Z
PART_REST = REST // 4

SEQ_PEERS = [
    (dy, dx, dc) for dy in (0, 3, 1, 2) for dx in (0, 1) for dc in (0, 1) if (dy, dx, dc) != (0, 0, 0)
]
CHIP_PEERS = [(0, 1), (1, 0), (3, 0), (1, 1), (3, 1), (2, 0), (2, 1)]


def dot(left, right):
    return lax.dot_general(left, right, (((1,), (0,)), ((), ())), preferred_element_type=F32)


def unpack_rope(x):
    return jnp.concatenate([x[:, :64], x[:, 64:]], axis=0)


def pack_rope(x):
    return jnp.concatenate([x[:64], x[64:]], axis=1)


def tile_of(lat, t, lo, hi):
    return jnp.concatenate([lat[0, t, lo:hi, :], lat[1, t, lo:hi, :]], axis=1)


def fused(
    seg, anc, qn_hbm, qr_hbm, lt_hbm, kr_hbm, uk_hbm, uv_hbm, g_hbm,
    ro, rw, fe,
    qn_in, qr_in, uk_in, uv_in, g_in,
    lat, sw, iw, sq, iq, wt, wtT, kcT, vT, kc, v, sc, dss, ps, qcs, gcs, dks, dvs, kvs, so, sdw, dl, ra, sa,
    rb, sb, rc, ry, sy, rz, part, other, whole,
    ins, own, l1s, l1r, l2s, l2r, l3s, l3r, iws, iwr, iqs, iqr, os, orr, ras, rar, rbs, rbr, rcs, rcr,
    rys, ryr, rzs, rzr, hs, hr, ws, wr, es, er,
):
    s, f = lax.axis_index("seq"), lax.axis_index("fsdp")
    y, x, c = s // 4, (s // 2) % 2, s % 2
    k = s // 2
    h, z = f // 4, f % 4

    def seq_peer(rel):
        return ((y + rel[0]) % 4) * 4 + ((x + rel[1]) % 2) * 2 + (c + rel[2]) % 2

    def chip_peer(rel):
        return ((y + rel[0]) % 4) * 2 + (x + rel[1]) % 2

    def z_peer(dz):
        return (z + dz) % 4

    other_core = (k * 2 + 1 - c, f)
    zrow = pl.multiple_of(z * PART, 16)

    def remote(src, dst, ssem, rsem, device):
        return pltpu.make_async_remote_copy(
            src_ref=src, dst_ref=dst, send_sem=ssem, recv_sem=rsem, device_id=device, device_id_type=MESH
        )

    loads = [
        pltpu.make_async_copy(src, dst, ins.at[i])
        for i, (src, dst) in enumerate(
            [
                (lt_hbm, lat.at[c, k, pl.ds(0, 512)]),
                (kr_hbm, lat.at[c, k, pl.ds(512, 64)]),
                (uk_hbm, uk_in),
                (uv_hbm, uv_in),
                (qn_hbm, qn_in),
                (qr_hbm, qr_in),
                (g_hbm, g_in),
            ]
        )
    ]
    for cp in loads:
        cp.start()

    bar = pltpu.get_barrier_semaphore()
    peers = [(seq_peer(r), f) for r in SEQ_PEERS]
    peers += [(s, h * 4 + z_peer(dz)) for dz in (1, 2, 3)]
    peers += [(s, (1 - h) * 4 + z)]
    for p in peers:
        pl.semaphore_signal(bar, inc=1, device_id=p, device_id_type=MESH)

    for cp in loads:
        cp.wait()
    for d in range(16):
        sw[d, 0:32, :] = uk_in[:, 128 * d : 128 * d + 128]
        sw[d, 32:64, :] = uv_in[:, 128 * d : 128 * d + 128]
        sq[d, 0:128, :] = qn_in[:, 128 * d : 128 * d + 128]
        sq[d, 192:320, :] = g_in[:, 128 * d : 128 * d + 128]
    for pair in range(8):
        both = qr_in[:, 128 * pair : 128 * pair + 128].astype(F32)
        sq[2 * pair, 128:192, :] = pack_rope(both[:, :64]).astype(BF16)
        sq[2 * pair + 1, 128:192, :] = pack_rope(both[:, 64:]).astype(BF16)
    iw[s] = sw[s]
    iq[s] = sq[s]
    pl.semaphore_wait(bar, len(peers))

    sends = []

    for i, r in enumerate(CHIP_PEERS):
        cp = remote(
            lat.at[c, k, pl.ds(zrow, PART)], lat.at[c, k, pl.ds(zrow, PART)],
            l1s.at[i], l1r.at[k], (chip_peer(r) * 2 + c, f),
        )
        cp.start()
        sends.append(cp)
    cp = remote(lat.at[c, k], lat.at[c, k], l3s.at[k], l3r.at[k], other_core)
    cp.start()
    sends.append(cp)
    for i, r in enumerate(CHIP_PEERS):
        q = chip_peer(r)
        piece = lat.at[c, q, pl.ds(zrow, PART)]
        remote(piece, piece, l1s.at[i], l1r.at[q], other_core).wait_recv()
        for j, dz in enumerate((1, 3, 2)):
            cp = remote(piece, piece, l2s.at[3 * i + j], l2r.at[4 * q + z], (s, h * 4 + z_peer(dz)))
            cp.start()
            sends.append(cp)
    for i, r in enumerate(SEQ_PEERS):
        p = seq_peer(r)
        cp = remote(sw.at[p], iw.at[s], iws.at[i], iwr.at[s], (p, f))
        cp.start()
        sends.append(cp)
    for i, r in enumerate(SEQ_PEERS):
        p = seq_peer(r)
        cp = remote(sq.at[p], iq.at[s], iqs.at[i], iqr.at[s], (p, f))
        cp.start()
        sends.append(cp)
    for r in SEQ_PEERS:
        p = seq_peer(r)
        remote(iw.at[p], iw.at[p], iws.at[0], iwr.at[p], other_core).wait_recv()
    for d in range(16):
        wt[0, 32 * d : 32 * d + 32, :] = iw[d, 0:32, :]
        wt[1, 32 * d : 32 * d + 32, :] = iw[d, 32:64, :]
    wtT[0:128, :] = wt[0].astype(F32).T.astype(BF16)
    wtT[128:256, :] = wt[1].astype(F32).T.astype(BF16)

    for i, r in enumerate(CHIP_PEERS):
        q = chip_peer(r)
        for dz in (1, 3, 2):
            zz = z_peer(dz)
            piece = lat.at[c, q, pl.ds(pl.multiple_of(zz * PART, 16), PART)]
            remote(piece, piece, l2s.at[0], l2r.at[4 * q + zz], other_core).wait_recv()
        cp = remote(lat.at[c, q], lat.at[c, q], l3s.at[q], l3r.at[q], other_core)
        cp.start()
        sends.append(cp)


    for r in [(0, 0)] + CHIP_PEERS:
        t = chip_peer(r)
        block = lat.at[1 - c, t]
        remote(block, block, l3s.at[0], l3r.at[t], other_core).wait_recv()
        rope = tile_of(lat, t, 512, 576)
        kv = dot(wtT[...], tile_of(lat, t, 0, 512))
        kcT[t, 0:128, :] = kv[:128].astype(BF16)
        kcT[t, 128:192, :] = rope
        vT[t] = kv[128:].astype(BF16)
        kc[t, :, 0:128] = kv[:128].T.astype(BF16)
        kc[t, :, 128:192] = rope.astype(F32).T.astype(BF16)
        v[t] = kv[128:].T.astype(BF16)

    lane = lax.broadcasted_iota(jnp.int32, (1, 256), 1)

    def bias_of(a, b):
        seen = (seg[128 * a] == seg[128 * b]) | (anc[a, b] == 1)
        return jnp.where(seen, 0.0, NEG).astype(F32)

    def pair_index(I, J):
        return I * (I + 1) // 2 + J

    def query_tile(I):
        a0, a1 = iq[2 * I], iq[2 * I + 1]
        qn = jnp.concatenate([a0[0:128], a1[0:128]], axis=0)
        g = jnp.concatenate([a0[192:320], a1[192:320]], axis=0)
        qr = jnp.concatenate(
            [unpack_rope(a0[128:192].astype(F32)), unpack_rope(a1[128:192].astype(F32))], axis=0
        )
        qT = jnp.concatenate([qn.astype(F32).T, qr.T], axis=0).astype(BF16)
        qcs[I] = jnp.concatenate([qn, qr.astype(BF16)], axis=1)
        gcs[I] = g
        gT = g.astype(F32).T
        top = jnp.full((1, 256), NEG, F32)
        for J in range(I + 1):
            scores = dot(kc[J], qT)
            if J < I:
                halves = []
                for b in range(2):
                    bias = jnp.where(
                        lane < 128, bias_of(2 * I, 2 * J + b), bias_of(2 * I + 1, 2 * J + b)
                    )
                    halves.append(scores[128 * b : 128 * b + 128] + bias)
                scores = jnp.concatenate(halves, axis=0)
            else:
                key = lax.broadcasted_iota(jnp.int32, (256, 256), 0)
                query = lax.broadcasted_iota(jnp.int32, (256, 256), 1)
                bias = jnp.where(lane < 128, 0.0, bias_of(2 * I + 1, 2 * I))
                scores = jnp.concatenate([scores[:128] + bias, scores[128:]], axis=0)
                scores = jnp.where(key <= query, scores, NEG)
            sc[J] = scores
            top = jnp.maximum(top, jnp.max(scores, axis=0, keepdims=True))
        top = top * SCALE_LOG2E
        total = jnp.zeros((1, 256), F32)
        oT = jnp.zeros((128, 256), F32)
        for J in range(I + 1):
            weight = jnp.exp2(sc[J] * SCALE_LOG2E - top)
            total = total + jnp.sum(weight, axis=0, keepdims=True)
            sc[J] = weight
            oT = oT + dot(vT[J], weight.astype(BF16))
        inverse = 1.0 / total
        oT = oT * inverse
        delta = jnp.sum(oT * gT, axis=0, keepdims=True)
        gT = gT.astype(BF16)
        dqT = jnp.zeros((192, 256), F32)
        for J in range(I + 1):
            prob = sc[J] * inverse
            ds = (prob * (dot(v[J], gT) - delta)).astype(BF16)
            dss[pair_index(I, J)] = ds
            ps[pair_index(I, J)] = prob.astype(BF16)
            dqT = dqT + dot(kcT[J], ds)
        dqT = dqT * SCALE
        o = oT.T.astype(BF16)
        dqn = dqT[:128].T.astype(BF16)
        dqr = dqT[128:].T
        for e in range(2):
            lo = 128 * e
            so[2 * I + e, 0:128, :] = o[lo : lo + 128]
            so[2 * I + e, 128:256, :] = dqn[lo : lo + 128]
            so[2 * I + e, 256:320, :] = pack_rope(dqr[lo : lo + 128]).astype(BF16)

    def backward_keys(J):
        dk = jnp.zeros((256, 192), F32)
        dv = jnp.zeros((256, 128), F32)
        for I in range(J, TILES):
            dk = dk + dot(dss[pair_index(I, J)], qcs[I])
            dv = dv + dot(ps[pair_index(I, J)], gcs[I])
        dk = dk * SCALE
        dks[...] = dk
        dvs[...] = dv

    def key_grads(J):
        dk = dks[...]
        kv = jnp.concatenate([dk[:, :128], dvs[...]], axis=1)
        kvs[J] = kv.astype(BF16)
        w = jnp.concatenate([wt[0], wt[1]], axis=1)
        lat_grad = dot(w, kv.T.astype(BF16)).astype(BF16)
        rope_grad = dk[:, 128:].T.astype(BF16)
        for e in range(2):
            dl[e, J, 0:512, :] = lat_grad[:, 128 * e : 128 * e + 128]
            dl[e, J, 512:576, :] = rope_grad[:, 128 * e : 128 * e + 128]
        remote(dl.at[1 - c, J], ra.at[J], ras.at[J], rar.at[J], other_core).start()

    def z_rows(base, size, zz):
        return pl.ds(pl.multiple_of(base + zz * size, 16), size)

    def add_cores(J):
        remote(ra.at[J], ra.at[J], ras.at[J], rar.at[J], other_core).wait_recv()
        sa[J] = (dl[c, J].astype(F32) + ra[J].astype(F32)).astype(BF16)
        for j, dz in enumerate((1, 3, 2)):
            zz = z_peer(dz)
            remote(
                sa.at[J, z_rows(0, PART_Z, zz)], rb.at[J, z], rbs.at[3 * J + j], rbr.at[4 * J + z], (s, h * 4 + zz)
            ).start()

        @pl.when(J != k)
        def _():
            remote(
                sa.at[J, pl.ds(ALONG_Z, REST)], ry.at[k], rys.at[J], ryr.at[k], (2 * J + c, f)
            ).start()

    def add_along_z(J):
        acc = sa[J, z_rows(0, PART_Z, z), :].astype(F32)
        for dz in (1, 3, 2):
            zz = z_peer(dz)
            remote(rb.at[J, zz], rb.at[J, zz], rbs.at[0], rbr.at[4 * J + zz], other_core).wait_recv()
            acc = acc + rb[J, zz].astype(F32)
        sb[J] = acc.astype(BF16)

    def tile_at(step):
        turn = step // 2
        dy = turn + (turn // 2) * (1 - 2 * (turn % 2))
        return ((y + dy) % 4) * 2 + (x + step) % 2

    def query_step(step, carry):
        tile = tile_at(step)
        for e in range(2):
            d = 2 * tile + e

            @pl.when(s != d)
            def _():
                remote(iq.at[d], iq.at[d], iqs.at[0], iqr.at[d], other_core).wait_recv()

        for I in range(TILES):

            @pl.when(tile == I)
            def _():
                query_tile(I)

        for e in range(2):
            d = 2 * tile + e

            @pl.when(s != d)
            def _():
                remote(so.at[d], ro.at[s], os.at[d], orr.at[s], (d, f)).start()

        return carry

    lax.fori_loop(0, TILES, query_step, 0)
    def key_step(step, carry):
        tile = tile_at(TILES - 1 - step)
        for J in range(TILES):

            @pl.when(tile == J)
            def _():
                backward_keys(J)

        key_grads(tile)

        @pl.when(step >= LAG)
        def _():
            add_cores(tile_at(TILES - 1 - step + LAG))

        @pl.when(step >= 2 * LAG)
        def _():
            add_along_z(tile_at(TILES - 1 - step + 2 * LAG))

        return carry

    lax.fori_loop(0, TILES, key_step, 0)
    w_grad = jnp.zeros((512, 256), F32)
    for t in range(TILES):
        w_grad = w_grad + dot(tile_of(lat, t, 0, 512), kvs[t])
    w_grad = w_grad.astype(BF16)
    for d in range(16):
        sdw[d, 0:32, :] = w_grad[32 * d : 32 * d + 32, :128]
        sdw[d, 32:64, :] = w_grad[32 * d : 32 * d + 32, 128:]
    for step in range(LAG - 1, -1, -1):
        add_cores(tile_at(step))
    for i, r in enumerate(SEQ_PEERS):
        p = seq_peer(r)
        cp = remote(sdw.at[p], rw.at[s], ws.at[i], wr.at[s], (p, f))
        cp.start()
        sends.append(cp)
    for step in range(2 * LAG - 1, -1, -1):
        add_along_z(tile_at(step))

    for i, r in enumerate(CHIP_PEERS):
        q = chip_peer(r)
        cp = remote(sb.at[q], rc.at[k], rcs.at[i], rcr.at[k], (2 * q + c, f))
        cp.start()
        sends.append(cp)
    acc = sa[k, ALONG_Z:576, :].astype(F32)
    for r in CHIP_PEERS:
        q = chip_peer(r)
        remote(ry.at[q], ry.at[q], rys.at[0], ryr.at[q], other_core).wait_recv()
        acc = acc + ry[q].astype(F32)
    sy[...] = acc.astype(BF16)
    for j, dz in enumerate((1, 3, 2)):
        zz = z_peer(dz)
        cp = remote(sy.at[z_rows(0, PART_REST, zz)], rz.at[z], rzs.at[j], rzr.at[z], (s, h * 4 + zz))
        cp.start()
        sends.append(cp)
    acc = sb[k].astype(F32)
    for r in CHIP_PEERS:
        q = chip_peer(r)
        remote(rc.at[q], rc.at[q], rcs.at[0], rcr.at[q], other_core).wait_recv()
        acc = acc + rc[q].astype(F32)
    part[0:PART_Z, :] = acc.astype(BF16)
    acc = sy[z_rows(0, PART_REST, z), :].astype(F32)
    for dz in (1, 3, 2):
        zz = z_peer(dz)
        remote(rz.at[zz], rz.at[zz], rzs.at[0], rzr.at[zz], other_core).wait_recv()
        acc = acc + rz[zz].astype(F32)
    part[PART_Z:PART, :] = acc.astype(BF16)
    cp = remote(part, other, hs.at[0], hr.at[0], (s, (1 - h) * 4 + z))
    cp.start()
    sends.append(cp)
    cp.wait_recv()
    whole[...] = (part[...].astype(F32) + other[...].astype(F32)).astype(BF16)
    for j, dz in enumerate((1, 3, 2)):
        cp = remote(whole, fe.at[z], es.at[j], er.at[z], (s, h * 4 + z_peer(dz)))
        cp.start()
        sends.append(cp)
    mine = [
        pltpu.make_async_copy(src, dst, own.at[i])
        for i, (src, dst) in enumerate(
            [(so.at[s], ro.at[s]), (sdw.at[s], rw.at[s]), (whole, fe.at[z])]
        )
    ]
    for cp in mine:
        cp.start()

    for r in SEQ_PEERS:
        p = seq_peer(r)
        remote(ro.at[p], ro.at[p], os.at[0], orr.at[p], other_core).wait_recv()
        remote(rw.at[p], rw.at[p], ws.at[0], wr.at[p], other_core).wait_recv()
        remote(so.at[p], so.at[p], os.at[p], orr.at[p], other_core).wait_send()
    for dz in (1, 3, 2):
        zz = z_peer(dz)
        remote(whole, fe.at[zz], es.at[0], er.at[zz], other_core).wait_recv()
    for cp in mine:
        cp.wait()
    for cp in sends:
        cp.wait_send()
    for J in range(TILES):
        remote(ra.at[J], ra.at[J], ras.at[J], rar.at[J], other_core).wait_send()
        for j in range(3):
            remote(rb.at[J, 0], rb.at[J, 0], rbs.at[3 * J + j], rbr.at[0], other_core).wait_send()

        @pl.when(J != k)
        def _():
            remote(ry.at[0], ry.at[0], rys.at[J], ryr.at[0], other_core).wait_send()


def unpack(
    ro_hbm, rw_hbm, fe_hbm, out, dqn, dqr, dlat, dkr, duk, duv, ro, rw, fe, sems
):
    loads = [
        pltpu.make_async_copy(src, dst, sems.at[i])
        for i, (src, dst) in enumerate([(ro_hbm, ro), (rw_hbm, rw), (fe_hbm, fe)])
    ]
    for cp in loads:
        cp.start()
    for cp in loads:
        cp.wait()
    for d in range(16):
        cols = slice(128 * d, 128 * d + 128)
        out[:, cols] = ro[d, 0:128, :]
        dqn[:, cols] = ro[d, 128:256, :]
        duk[:, cols] = rw[d, 0:32, :].astype(F32)
        duv[:, cols] = rw[d, 32:64, :].astype(F32)
    for pair in range(8):
        both = [unpack_rope(ro[2 * pair + e, 256:320, :].astype(F32)) for e in range(2)]
        dqr[:, 128 * pair : 128 * pair + 128] = jnp.concatenate(both, axis=1).astype(BF16)
    for z in range(4):
        dlat[PART_Z * z : PART_Z * z + PART_Z, :] = fe[z, 0:PART_Z, :]
        rest = fe[z, PART_Z:PART, :]
        lo = ALONG_Z + PART_REST * z
        if lo < 512:
            dlat[lo : lo + PART_REST, :] = rest
        else:
            dkr[lo - 512 : lo - 512 + PART_REST, :] = rest


def on_device(q_nope, q_rope, latent_t, k_rope_t, w_uk, w_uv, grad_out, seg_ids, anc_flags):
    vmem = pl.BlockSpec(memory_space=pltpu.VMEM)
    smem = pl.BlockSpec(memory_space=pltpu.SMEM)
    anywhere = pl.BlockSpec(memory_space=pl.ANY)
    dma = pltpu.SemaphoreType.DMA
    sem_counts = [7, 3, 7, 8, 21, 32, 8, 8, 15, 16, 15, 16, 16, 16, 8, 8, 24, 32, 7, 8]
    sem_counts += [8, 8, 3, 4, 1, 1, 15, 16, 3, 4]
    parts = pl.pallas_call(
        fused,
        out_shape=[
            jax.ShapeDtypeStruct((16, 320, 128), BF16),
            jax.ShapeDtypeStruct((16, 64, 128), BF16),
            jax.ShapeDtypeStruct((4, PART, 128), BF16),
        ],
        in_specs=[smem, smem] + [anywhere] * 7,
        out_specs=[anywhere] * 3,
        scratch_shapes=[
            pltpu.VMEM((128, 2048), BF16),
            pltpu.VMEM((128, 1024), BF16),
            pltpu.VMEM((32, 2048), BF16),
            pltpu.VMEM((32, 2048), BF16),
            pltpu.VMEM((128, 2048), BF16),
            pltpu.VMEM((2, 8, 576, 128), BF16),
            pltpu.VMEM((16, 64, 128), BF16),
            pltpu.VMEM((16, 64, 128), BF16),
            pltpu.VMEM((16, 320, 128), BF16),
            pltpu.VMEM((16, 320, 128), BF16),
            pltpu.VMEM((2, 512, 128), BF16),
            pltpu.VMEM((256, 512), BF16),
            pltpu.VMEM((8, 192, 256), BF16),
            pltpu.VMEM((8, 128, 256), BF16),
            pltpu.VMEM((8, 256, 192), BF16),
            pltpu.VMEM((8, 256, 128), BF16),
            pltpu.VMEM((8, 256, 256), F32),
            pltpu.VMEM((36, 256, 256), BF16),
            pltpu.VMEM((36, 256, 256), BF16),
            pltpu.VMEM((8, 256, 192), BF16),
            pltpu.VMEM((8, 256, 128), BF16),
            pltpu.VMEM((256, 192), F32),
            pltpu.VMEM((256, 128), F32),
            pltpu.VMEM((8, 256, 256), BF16),
            pltpu.VMEM((16, 320, 128), BF16),
            pltpu.VMEM((16, 64, 128), BF16),
            pltpu.VMEM((2, 8, 576, 128), BF16),
            pltpu.VMEM((8, 576, 128), BF16),
            pltpu.VMEM((8, 576, 128), BF16),
            pltpu.VMEM((8, 4, PART_Z, 128), BF16),
            pltpu.VMEM((8, PART_Z, 128), BF16),
            pltpu.VMEM((8, PART_Z, 128), BF16),
            pltpu.VMEM((8, REST, 128), BF16),
            pltpu.VMEM((REST, 128), BF16),
            pltpu.VMEM((4, PART_REST, 128), BF16),
            pltpu.VMEM((PART, 128), BF16),
            pltpu.VMEM((PART, 128), BF16),
            pltpu.VMEM((PART, 128), BF16),
        ]
        + [dma((n,)) for n in sem_counts],
        compiler_params=pltpu.CompilerParams(
            collective_id=0, has_side_effects=True, vmem_limit_bytes=56 * 1024 * 1024
        ),
        name="attention_exchange",
    )(seg_ids, anc_flags, q_nope, q_rope, latent_t, k_rope_t, w_uk, w_uv, grad_out)
    bf, fl = BF16, F32
    return pl.pallas_call(
        unpack,
        out_shape=[
            jax.ShapeDtypeStruct((128, 2048), bf),
            jax.ShapeDtypeStruct((128, 2048), bf),
            jax.ShapeDtypeStruct((128, 1024), bf),
            jax.ShapeDtypeStruct((512, 128), bf),
            jax.ShapeDtypeStruct((64, 128), bf),
            jax.ShapeDtypeStruct((32, 2048), fl),
            jax.ShapeDtypeStruct((32, 2048), fl),
        ],
        in_specs=[anywhere] * 3,
        out_specs=[vmem] * 7,
        scratch_shapes=[
            pltpu.VMEM((16, 320, 128), bf),
            pltpu.VMEM((16, 64, 128), bf),
            pltpu.VMEM((4, PART, 128), bf),
            dma((3,)),
        ],
        compiler_params=pltpu.CompilerParams(vmem_limit_bytes=60 * 1024 * 1024),
        name="unpack",
    )(*parts)


def solution(mesh):
    placed = (
        P("seq", "fsdp"),
        P("seq", "fsdp"),
        P(None, "seq"),
        P(None, "seq"),
        P("seq", "fsdp"),
        P("seq", "fsdp"),
        P("seq", "fsdp"),
        P(),
        P(),
    )
    return jax.shard_map(
        on_device,
        mesh=mesh,
        in_specs=placed,
        out_specs=(
            P("seq", "fsdp"),
            P("seq", "fsdp"),
            P("seq", "fsdp"),
            P(None, "seq"),
            P(None, "seq"),
            P("seq", "fsdp"),
            P("seq", "fsdp"),
        ),
        check_vma=False,
    )
```

time: 89.9 us -> 79 us (0.88)
  Pallas kernels: 85.8 us -> 77.9 us
  local copies, waits for them, and re-layouts: 3.17 us -> 0 us
    pallas_call x1, Pallas kernels: 84.2 us -> 74.9 us  [on_device(): pl.pallas_call(fused, out_shape=[jax.ShapeDtypeStruct((16, 320, 128), BF1...]
    unnamed x6 -> x0, local copies, waits for them, and re-layouts: 3.17 us -> none
    pallas_call x1, Pallas kernels: 1.59 us -> 3 us  [on_device(): pl.pallas_call(unpack, out_shape=[jax.ShapeDtypeStruct((128, 2048), bf),...]
where the time goes in v2:
time: 79 us; the launch traced here: 78.8 us
  Pallas kernels  77.9 us (99%)
  between operations  0.82 us (1%)
    pallas_call x1, Pallas kernels, on_device(): pl.pallas_call(fused, out_shape=[jax.ShapeDtypeStruct((16, 320, 128), BF1...  74.9 us
    pallas_call x1, Pallas kernels, on_device(): pl.pallas_call(unpack, out_shape=[jax.ShapeDtypeStruct((128, 2048), bf),...  3 us

profile of v2, /device:TPU:0, one launch (start us, length us, event | category | flops | bytes accessed | tf_op | source)
XLA Modules:
  0.0 78.8 jit_solution(1457107925915780194)
XLA Ops:
  0.6 74.9 %attention_exchange.1 = (bf16[16,320,128]{2,1,0:T(8,128)(2,1)}, bf16[16,64,128]{2,1,0:T(8,128)(2,1)}, bf16[4,144,128]{2,1,0:T(8,128)(2,1)}) custom-call(s32[2048]{0:T(1024)} %seg.1, s32[16,16]{1,0:T(8,128)} %anc.1, bf16[128,2048]{1,0:T(8,128)(2,1)} %qn_hbm.1, bf16[128,1024]{1,0:T(8,128)(2,1)} %qr_hbm.1, bf16[512,128]{1,0:T(8,128)(2,1)} %lt_hbm.1, ...), custom_call_target="tpu_custom_call" | custom-call | tf_op jit(solution)/shard_map/attention_exchange/pallas_call | solution.py:468
  75.6 3.0 %unpack.1 = (bf16[128,2048]{1,0:T(8,128)(2,1)}, bf16[128,2048]{1,0:T(8,128)(2,1)}, bf16[128,1024]{1,0:T(8,128)(2,1)}, bf16[512,128]{1,0:T(8,128)(2,1)}, bf16[64,...) custom-call(bf16[16,320,128]{2,1,0:T(8,128)(2,1)} %get-tuple-element.10.ro_hbm, ...), custom_call_target="tpu_custom_call" | custom-call | tf_op jit(solution)/shard_map/unpack/pallas_call | solution.py:524

commit v3 on v2

--- a/solution.py
+++ b/solution.py
@@ -14,17 +14,17 @@
 SCALE = 1.0 / math.sqrt(192.0)
 SCALE_LOG2E = SCALE * math.log2(math.e)
 TILES = 8
-LAG = 2
+LAG = 3
+LAT_Z = 512
+LAT_PART = LAT_Z // 4
 PART = 144
-ALONG_Z = 448
+ALONG_Z = 320
 PART_Z = ALONG_Z // 4
 REST = 576 - ALONG_Z
 PART_REST = REST // 4
 
-SEQ_PEERS = [
-    (dy, dx, dc) for dy in (0, 3, 1, 2) for dx in (0, 1) for dc in (0, 1) if (dy, dx, dc) != (0, 0, 0)
-]
-CHIP_PEERS = [(0, 1), (1, 0), (3, 0), (1, 1), (3, 1), (2, 0), (2, 1)]
+SEQ_PEERS = [(dy, dx, dc) for dy in (0, 3, 1, 2) for dx in (0, 1) for dc in (0, 1)][1:]
+CHIP_PEERS = [(0, 1), (1, 0), (3, 0), (2, 0), (1, 1), (3, 1), (2, 1)]
 
 
 def dot(left, right):
@@ -49,7 +49,7 @@
     qn_in, qr_in, uk_in, uv_in, g_in,
     lat, sw, iw, sq, iq, wt, wtT, kcT, vT, kc, v, sc, dss, ps, qcs, gcs, dks, dvs, kvs, so, sdw, dl, ra, sa,
     rb, sb, rc, ry, sy, rz, part, other, whole,
-    ins, own, l1s, l1r, l2s, l2r, l3s, l3r, iws, iwr, iqs, iqr, os, orr, ras, rar, rbs, rbr, rcs, rcr,
+    ins, own, l1s, l1r, lds, ldr, l2s, l2r, l3s, l3r, iws, iwr, iqs, iqr, os, orr, ras, rar, rbs, rbr, rcs, rcr,
     rys, ryr, rzs, rzr, hs, hr, ws, wr, es, er,
 ):
     s, f = lax.axis_index("seq"), lax.axis_index("fsdp")
@@ -67,7 +67,7 @@
         return (z + dz) % 4
 
     other_core = (k * 2 + 1 - c, f)
-    zrow = pl.multiple_of(z * PART, 16)
+    zrow = pl.multiple_of(z * LAT_PART, 16)
 
     def remote(src, dst, ssem, rsem, device):
         return pltpu.make_async_remote_copy(
@@ -115,37 +115,47 @@
 
     sends = []
 
+    mine = lat.at[c, k, pl.ds(zrow, LAT_PART)]
+    rest = lat.at[c, k, pl.ds(LAT_Z, 576 - LAT_Z)]
     for i, r in enumerate(CHIP_PEERS):
-        cp = remote(
-            lat.at[c, k, pl.ds(zrow, PART)], lat.at[c, k, pl.ds(zrow, PART)],
-            l1s.at[i], l1r.at[k], (chip_peer(r) * 2 + c, f),
-        )
+        cp = remote(mine, mine, l1s.at[i], l1r.at[k], (chip_peer(r) * 2 + c, f))
+        cp.start()
+        sends.append(cp)
+    for i, r in enumerate(CHIP_PEERS):
+        cp = remote(rest, rest, lds.at[i], ldr.at[k], (chip_peer(r) * 2 + c, f))
         cp.start()
         sends.append(cp)
     cp = remote(lat.at[c, k], lat.at[c, k], l3s.at[k], l3r.at[k], other_core)
     cp.start()
     sends.append(cp)
+    for i, r in enumerate(SEQ_PEERS):
+        p = seq_peer(r)
+        cp = remote(sw.at[p], iw.at[s], iws.at[i], iwr.at[s], (p, f))
+        cp.start()
+        sends.append(cp)
     for i, r in enumerate(CHIP_PEERS):
         q = chip_peer(r)
-        piece = lat.at[c, q, pl.ds(zrow, PART)]
+        piece = lat.at[c, q, pl.ds(zrow, LAT_PART)]
         remote(piece, piece, l1s.at[i], l1r.at[q], other_core).wait_recv()
         for j, dz in enumerate((1, 3, 2)):
             cp = remote(piece, piece, l2s.at[3 * i + j], l2r.at[4 * q + z], (s, h * 4 + z_peer(dz)))
             cp.start()
             sends.append(cp)
-    for i, r in enumerate(SEQ_PEERS):
-        p = seq_peer(r)
-        cp = remote(sw.at[p], iw.at[s], iws.at[i], iwr.at[s], (p, f))
-        cp.start()
-        sends.append(cp)
-    for i, r in enumerate(SEQ_PEERS):
-        p = seq_peer(r)
-        cp = remote(sq.at[p], iq.at[s], iqs.at[i], iqr.at[s], (p, f))
-        cp.start()
-        sends.append(cp)
+    for r in CHIP_PEERS:
+        block = lat.at[c, chip_peer(r), pl.ds(LAT_Z, 576 - LAT_Z)]
+        remote(block, block, lds.at[0], ldr.at[chip_peer(r)], other_core).wait_recv()
     for r in SEQ_PEERS:
         p = seq_peer(r)
         remote(iw.at[p], iw.at[p], iws.at[0], iwr.at[p], other_core).wait_recv()
+
+    def send_queries(peers):
+        for i in peers:
+            for e in range(2):
+                p = chip_peer(CHIP_PEERS[i]) * 2 + e
+                remote(sq.at[p], iq.at[s], iqs.at[2 * i + e], iqr.at[s], (p, f)).start()
+
+    remote(sq.at[k * 2 + 1 - c], iq.at[s], iqs.at[14], iqr.at[s], other_core).start()
+    send_queries(range(7))
     for d in range(16):
         wt[0, 32 * d : 32 * d + 32, :] = iw[d, 0:32, :]
         wt[1, 32 * d : 32 * d + 32, :] = iw[d, 32:64, :]
@@ -156,7 +166,7 @@
         q = chip_peer(r)
         for dz in (1, 3, 2):
             zz = z_peer(dz)
-            piece = lat.at[c, q, pl.ds(pl.multiple_of(zz * PART, 16), PART)]
+            piece = lat.at[c, q, pl.ds(pl.multiple_of(zz * LAT_PART, 16), LAT_PART)]
             remote(piece, piece, l2s.at[0], l2r.at[4 * q + zz], other_core).wait_recv()
         cp = remote(lat.at[c, q], lat.at[c, q], l3s.at[q], l3r.at[q], other_core)
         cp.start()
@@ -293,9 +303,11 @@
         sb[J] = acc.astype(BF16)
 
     def tile_at(step):
-        turn = step // 2
-        dy = turn + (turn // 2) * (1 - 2 * (turn % 2))
-        return ((y + dy) % 4) * 2 + (x + step) % 2
+        far = (step + 6) // 8
+        turn = (step + 1) % 3
+        dy = far * (1 + 2 * turn - 3 * (turn // 2))
+        dx = (1 - far) * step + far * ((step + 1) // 3 - 1)
+        return ((y + dy) % 4) * 2 + (x + dx) % 2
 
     def query_step(step, carry):
         tile = tile_at(step)
@@ -397,13 +409,13 @@
         cp = remote(whole, fe.at[z], es.at[j], er.at[z], (s, h * 4 + z_peer(dz)))
         cp.start()
         sends.append(cp)
-    mine = [
+    kept = [
         pltpu.make_async_copy(src, dst, own.at[i])
         for i, (src, dst) in enumerate(
             [(so.at[s], ro.at[s]), (sdw.at[s], rw.at[s]), (whole, fe.at[z])]
         )
     ]
-    for cp in mine:
+    for cp in kept:
         cp.start()
 
     for r in SEQ_PEERS:
@@ -414,10 +426,12 @@
     for dz in (1, 3, 2):
         zz = z_peer(dz)
         remote(whole, fe.at[zz], es.at[0], er.at[zz], other_core).wait_recv()
-    for cp in mine:
+    for cp in kept:
         cp.wait()
     for cp in sends:
         cp.wait_send()
+    for i in range(15):
+        remote(sq.at[0], sq.at[0], iqs.at[i], iqr.at[0], other_core).wait_send()
     for J in range(TILES):
         remote(ra.at[J], ra.at[J], ras.at[J], rar.at[J], other_core).wait_send()
         for j in range(3):
@@ -463,7 +477,7 @@
     smem = pl.BlockSpec(memory_space=pltpu.SMEM)
     anywhere = pl.BlockSpec(memory_space=pl.ANY)
     dma = pltpu.SemaphoreType.DMA
-    sem_counts = [7, 3, 7, 8, 21, 32, 8, 8, 15, 16, 15, 16, 16, 16, 8, 8, 24, 32, 7, 8]
+    sem_counts = [7, 3, 7, 8, 7, 8, 21, 32, 8, 8, 15, 16, 15, 16, 16, 16, 8, 8, 24, 32, 7, 8]
     sem_counts += [8, 8, 3, 4, 1, 1, 15, 16, 3, 4]
     parts = pl.pallas_call(
         fused,

time: 79 us -> 76.4 us (0.967)
  Pallas kernels: 77.9 us -> 75.3 us
    pallas_call x1, Pallas kernels: 74.9 us -> 72.3 us  [on_device(): pl.pallas_call(fused, out_shape=[jax.ShapeDtypeStruct((16, 320, 128), BF1...]
where the time goes in v3:
time: 76.4 us; the launch traced here: 76.1 us
  Pallas kernels  75.3 us (99%)
  between operations  0.82 us (1%)
    pallas_call x1, Pallas kernels, on_device(): pl.pallas_call(fused, out_shape=[jax.ShapeDtypeStruct((16, 320, 128), BF1...  72.3 us
    pallas_call x1, Pallas kernels, on_device(): pl.pallas_call(unpack, out_shape=[jax.ShapeDtypeStruct((128, 2048), bf),...  3 us

profile of v3, /device:TPU:0, one launch (start us, length us, event | category | flops | bytes accessed | tf_op | source)
XLA Modules:
  0.0 76.1 jit_solution(13990384355760133644)
XLA Ops:
  0.6 72.3 %attention_exchange.1 = (bf16[16,320,128]{2,1,0:T(8,128)(2,1)}, bf16[16,64,128]{2,1,0:T(8,128)(2,1)}, bf16[4,144,128]{2,1,0:T(8,128)(2,1)}) custom-call(s32[2048]{0:T(1024)} %seg.1, s32[16,16]{1,0:T(8,128)} %anc.1, bf16[128,2048]{1,0:T(8,128)(2,1)} %qn_hbm.1, bf16[128,1024]{1,0:T(8,128)(2,1)} %qr_hbm.1, bf16[512,128]{1,0:T(8,128)(2,1)} %lt_hbm.1, ...), custom_call_target="tpu_custom_call" | custom-call | tf_op jit(solution)/shard_map/attention_exchange/pallas_call | solution.py:482
  73.0 3.0 %unpack.1 = (bf16[128,2048]{1,0:T(8,128)(2,1)}, bf16[128,2048]{1,0:T(8,128)(2,1)}, bf16[128,1024]{1,0:T(8,128)(2,1)}, bf16[512,128]{1,0:T(8,128)(2,1)}, bf16[64,...) custom-call(bf16[16,320,128]{2,1,0:T(8,128)(2,1)} %get-tuple-element.10.ro_hbm, ...), custom_call_target="tpu_custom_call" | custom-call | tf_op jit(solution)/shard_map/unpack/pallas_call | solution.py:538

commit v4 on v3

--- a/solution.py
+++ b/solution.py
@@ -141,6 +141,14 @@
             cp = remote(piece, piece, l2s.at[3 * i + j], l2r.at[4 * q + z], (s, h * 4 + z_peer(dz)))
             cp.start()
             sends.append(cp)
+    def send_queries(peers):
+        for i in peers:
+            for e in range(2):
+                p = chip_peer(CHIP_PEERS[i]) * 2 + e
+                remote(sq.at[p], iq.at[s], iqs.at[2 * i + e], iqr.at[s], (p, f)).start()
+
+    remote(sq.at[k * 2 + 1 - c], iq.at[s], iqs.at[14], iqr.at[s], other_core).start()
+    send_queries(range(7))
     for r in CHIP_PEERS:
         block = lat.at[c, chip_peer(r), pl.ds(LAT_Z, 576 - LAT_Z)]
         remote(block, block, lds.at[0], ldr.at[chip_peer(r)], other_core).wait_recv()
@@ -148,14 +156,6 @@
         p = seq_peer(r)
         remote(iw.at[p], iw.at[p], iws.at[0], iwr.at[p], other_core).wait_recv()
 
-    def send_queries(peers):
-        for i in peers:
-            for e in range(2):
-                p = chip_peer(CHIP_PEERS[i]) * 2 + e
-                remote(sq.at[p], iq.at[s], iqs.at[2 * i + e], iqr.at[s], (p, f)).start()
-
-    remote(sq.at[k * 2 + 1 - c], iq.at[s], iqs.at[14], iqr.at[s], other_core).start()
-    send_queries(range(7))
     for d in range(16):
         wt[0, 32 * d : 32 * d + 32, :] = iw[d, 0:32, :]
         wt[1, 32 * d : 32 * d + 32, :] = iw[d, 32:64, :]

time: 76.4 us -> 75 us (0.982)
  Pallas kernels: 75.3 us -> 74 us
    pallas_call x1, Pallas kernels: 72.3 us -> 71 us  [on_device(): pl.pallas_call(fused, out_shape=[jax.ShapeDtypeStruct((16, 320, 128), BF1...]
where the time goes in v4:
time: 75 us; the launch traced here: 74.8 us
  Pallas kernels  74 us (99%)
  between operations  0.82 us (1%)
    pallas_call x1, Pallas kernels, on_device(): pl.pallas_call(fused, out_shape=[jax.ShapeDtypeStruct((16, 320, 128), BF1...  71 us
    pallas_call x1, Pallas kernels, on_device(): pl.pallas_call(unpack, out_shape=[jax.ShapeDtypeStruct((128, 2048), bf),...  3 us

profile of v4, /device:TPU:0, one launch (start us, length us, event | category | flops | bytes accessed | tf_op | source)
XLA Modules:
  0.0 74.8 jit_solution(8401314688246884954)
XLA Ops:
  0.6 71.0 %attention_exchange.1 = (bf16[16,320,128]{2,1,0:T(8,128)(2,1)}, bf16[16,64,128]{2,1,0:T(8,128)(2,1)}, bf16[4,144,128]{2,1,0:T(8,128)(2,1)}) custom-call(s32[2048]{0:T(1024)} %seg.1, s32[16,16]{1,0:T(8,128)} %anc.1, bf16[128,2048]{1,0:T(8,128)(2,1)} %qn_hbm.1, bf16[128,1024]{1,0:T(8,128)(2,1)} %qr_hbm.1, bf16[512,128]{1,0:T(8,128)(2,1)} %lt_hbm.1, ...), custom_call_target="tpu_custom_call" | custom-call | tf_op jit(solution)/shard_map/attention_exchange/pallas_call | solution.py:482
  71.6 3.0 %unpack.1 = (bf16[128,2048]{1,0:T(8,128)(2,1)}, bf16[128,2048]{1,0:T(8,128)(2,1)}, bf16[128,1024]{1,0:T(8,128)(2,1)}, bf16[512,128]{1,0:T(8,128)(2,1)}, bf16[64,...) custom-call(bf16[16,320,128]{2,1,0:T(8,128)(2,1)} %get-tuple-element.10.ro_hbm, ...), custom_call_target="tpu_custom_call" | custom-call | tf_op jit(solution)/shard_map/unpack/pallas_call | solution.py:538

commit v5 on v4

--- a/solution.py
+++ b/solution.py
@@ -445,23 +445,18 @@
 def unpack(
     ro_hbm, rw_hbm, fe_hbm, out, dqn, dqr, dlat, dkr, duk, duv, ro, rw, fe, sems
 ):
-    loads = [
-        pltpu.make_async_copy(src, dst, sems.at[i])
-        for i, (src, dst) in enumerate([(ro_hbm, ro), (rw_hbm, rw), (fe_hbm, fe)])
-    ]
+    loads = [pltpu.make_async_copy(rw_hbm, rw, sems.at[0]), pltpu.make_async_copy(fe_hbm, fe, sems.at[1])]
+    for part in range(4):
+        heads = pl.ds(4 * part, 4)
+        loads.append(pltpu.make_async_copy(ro_hbm.at[heads], ro.at[heads], sems.at[2 + part]))
     for cp in loads:
         cp.start()
-    for cp in loads:
-        cp.wait()
+    loads[0].wait()
     for d in range(16):
         cols = slice(128 * d, 128 * d + 128)
-        out[:, cols] = ro[d, 0:128, :]
-        dqn[:, cols] = ro[d, 128:256, :]
         duk[:, cols] = rw[d, 0:32, :].astype(F32)
         duv[:, cols] = rw[d, 32:64, :].astype(F32)
-    for pair in range(8):
-        both = [unpack_rope(ro[2 * pair + e, 256:320, :].astype(F32)) for e in range(2)]
-        dqr[:, 128 * pair : 128 * pair + 128] = jnp.concatenate(both, axis=1).astype(BF16)
+    loads[1].wait()
     for z in range(4):
         dlat[PART_Z * z : PART_Z * z + PART_Z, :] = fe[z, 0:PART_Z, :]
         rest = fe[z, PART_Z:PART, :]
@@ -470,6 +465,15 @@
             dlat[lo : lo + PART_REST, :] = rest
         else:
             dkr[lo - 512 : lo - 512 + PART_REST, :] = rest
+    for part in range(4):
+        loads[2 + part].wait()
+        for d in range(4 * part, 4 * part + 4):
+            cols = slice(128 * d, 128 * d + 128)
+            out[:, cols] = ro[d, 0:128, :]
+            dqn[:, cols] = ro[d, 128:256, :]
+        for pair in range(2 * part, 2 * part + 2):
+            both = [unpack_rope(ro[2 * pair + e, 256:320, :].astype(F32)) for e in range(2)]
+            dqr[:, 128 * pair : 128 * pair + 128] = jnp.concatenate(both, axis=1).astype(BF16)
 
 
 def on_device(q_nope, q_rope, latent_t, k_rope_t, w_uk, w_uv, grad_out, seg_ids, anc_flags):
@@ -552,7 +556,7 @@
             pltpu.VMEM((16, 320, 128), bf),
             pltpu.VMEM((16, 64, 128), bf),
             pltpu.VMEM((4, PART, 128), bf),
-            dma((3,)),
+            dma((6,)),
         ],
         compiler_params=pltpu.CompilerParams(vmem_limit_bytes=60 * 1024 * 1024),
         name="unpack",

time: 75 us -> 75.2 us (level)
  no operation moved by 1% of the time
where the time goes in v5:
time: 75.2 us; the launch traced here: 75 us
  Pallas kernels  74.1 us (99%)
  between operations  0.82 us (1%)
    pallas_call x1, Pallas kernels, on_device(): pl.pallas_call(fused, out_shape=[jax.ShapeDtypeStruct((16, 320, 128), BF1...  71 us
    pallas_call x1, Pallas kernels, on_device(): pl.pallas_call(unpack, out_shape=[jax.ShapeDtypeStruct((128, 2048), bf),...  3.17 us

profile of v5, /device:TPU:0, one launch (start us, length us, event | category | flops | bytes accessed | tf_op | source)
XLA Modules:
  0.0 75.0 jit_solution(12173435308012726018)
XLA Ops:
  0.6 71.0 %attention_exchange.1 = (bf16[16,320,128]{2,1,0:T(8,128)(2,1)}, bf16[16,64,128]{2,1,0:T(8,128)(2,1)}, bf16[4,144,128]{2,1,0:T(8,128)(2,1)}) custom-call(s32[2048]{0:T(1024)} %seg.1, s32[16,16]{1,0:T(8,128)} %anc.1, bf16[128,2048]{1,0:T(8,128)(2,1)} %qn_hbm.1, bf16[128,1024]{1,0:T(8,128)(2,1)} %qr_hbm.1, bf16[512,128]{1,0:T(8,128)(2,1)} %lt_hbm.1, ...), custom_call_target="tpu_custom_call" | custom-call | tf_op jit(solution)/shard_map/attention_exchange/pallas_call | solution.py:486
  71.6 3.2 %unpack.1 = (bf16[128,2048]{1,0:T(8,128)(2,1)}, bf16[128,2048]{1,0:T(8,128)(2,1)}, bf16[128,1024]{1,0:T(8,128)(2,1)}, bf16[512,128]{1,0:T(8,128)(2,1)}, bf16[64,...) custom-call(bf16[16,320,128]{2,1,0:T(8,128)(2,1)} %get-tuple-element.10.ro_hbm, ...), custom_call_target="tpu_custom_call" | custom-call | tf_op jit(solution)/shard_map/unpack/pallas_call | solution.py:542
